TPU v7x, 512 devices: a whole 4x8x8 slice. The times are simulated.
512 devices in a mesh: blk: 128 (over z, y, core), col: 4 (over x).
Axes of the slice: x: 4, y: 8, z: 8, core: 2. Of those that a mesh axis runs over, the one named last changes fastest.
Arguments:
- coords: float32 [1024, 2, 128], P('blk'), may hold values from -0.125 to 1.125, as said below
- neighbours: int32 [1024, 4], P('blk'), may hold values from -1 to 1023, as said below
- sections: int32 [1024], P('blk'), may hold values from 0 to 7, as said below
- normals: float32 [16, 131072], P('col', 'blk'), may hold values from -6 to 6
Outputs:
- samples: float32 [16, 131072], P('col', 'blk')
Inputs may be any that keep to these rules, and one draw needn't show every extreme that they name: `neighbours`: every listed block has a lower section than the block that lists it; no block is listed twice in one row; blocks of section 0 list -1 only, other blocks list -1 only where fewer than 4 blocks of lower section exist. `sections`: among the 8 blocks of one device at most 2 share a section, and on every device exactly 2 do. `coords`: the points of one block lie in a small square around a centre in the unit square.
All inputs are finite; a program needn't handle non-finite values.
Results may differ from a plain program's by a relative error of at most 0.0003.
Values sent between devices are 32-bit elements; how exact they have to be, the bound alone decides.
A program may use at most 64 MiB of HBM per device.

v0:
```python
import jax
import jax.numpy as jnp
from jax import lax
from jax.sharding import PartitionSpec as P

K = 4
SECTIONS = 8
CAP = 2


length_scale = 0.5
nugget_var = 0.1


def covariance_kernel(left_pts, right_pts):
    delta_x = left_pts[0][:, None] - right_pts[0][None, :]
    delta_y = left_pts[1][:, None] - right_pts[1][None, :]
    return jnp.exp(-jnp.sqrt(delta_x * delta_x + delta_y * delta_y) / length_scale)


def factor(own_pts, near_pts, present):
    points = own_pts.shape[1]
    near_cov = covariance_kernel(near_pts, near_pts) * (present[:, None] * present[None, :])
    near_cov = near_cov + jnp.diag(nugget_var * present + (1.0 - present))
    cross_cov = covariance_kernel(own_pts, near_pts) * present[None, :]
    self_cov = covariance_kernel(own_pts, own_pts) + nugget_var * jnp.eye(points, dtype=jnp.float32)
    chol_near = jnp.linalg.cholesky(near_cov)
    whitened = lax.linalg.triangular_solve(chol_near, cross_cov.T, left_side=True, lower=True)
    cond_cov = self_cov - jnp.dot(whitened.T, whitened, precision=lax.Precision.HIGHEST)
    weight_t = lax.linalg.triangular_solve(
        chol_near, whitened, left_side=True, lower=True, transpose_a=True
    )
    return (weight_t.T, jnp.linalg.cholesky(cond_cov))


def assemble_every_factor(inputs):
    return lax.map(lambda triple: factor(triple[0], triple[1], triple[2]), inputs)


def local(coords, neighbours, sections, normals):
    resident_block_list = coords.shape[0]
    points = coords.shape[2]
    columns = normals.shape[0]
    col_count = lax.axis_size("col")
    slot_ids = jnp.arange(resident_block_list, dtype=jnp.int32)
    earlier = (sections[None, :] == sections[:, None]) & (slot_ids[None, :] < slot_ids[:, None])
    within = jnp.sum(earlier.astype(jnp.int32), axis=1)
    section_rank = jnp.stack([sections, within], axis=1)
    flat_ids = neighbours.reshape(-1)
    entries = flat_ids.shape[0]
    start_pick = (jnp.zeros((entries, 2 * points), jnp.float32), jnp.zeros((entries, 2), jnp.int32))
    part_coords = lax.all_gather(coords, "blk", axis=0, tiled=True)
    part_info = lax.all_gather(section_rank, "blk", axis=0, tiled=True)
    count_now = part_coords.shape[0]
    matches = flat_ids[:, None] == jnp.arange(count_now, dtype=jnp.int32)[None, :]
    moved = jnp.dot(
        matches.astype(jnp.float32),
        part_coords.reshape(count_now, 2 * points),
        precision=lax.Precision.HIGHEST,
    )
    info_add = jnp.sum(matches.astype(jnp.int32)[:, :, None] * part_info[None, :, :], axis=1)
    near_info = start_pick[1] + info_add
    present_k = flat_ids >= 0
    near_section = jnp.where(present_k, near_info[:, 0], -1)
    slot_key = jnp.clip(
        flat_ids // resident_block_list * CAP + near_info[:, 1], 0, lax.axis_size("blk") * CAP - 1
    )
    near_pts = jnp.transpose(
        moved.reshape(resident_block_list, K, 2, points), (0, 2, 1, 3)
    ).reshape(resident_block_list, 2, K * points)
    present = jnp.repeat(
        present_k.astype(jnp.float32).reshape(resident_block_list, K), points, axis=1
    )
    per_col = resident_block_list // col_count
    first_block = lax.axis_index("col") * per_col
    own_part = lax.dynamic_slice_in_dim(coords, first_block, per_col, 0)
    near_part = lax.dynamic_slice_in_dim(near_pts, first_block, per_col, 0)
    mask_part = lax.dynamic_slice_in_dim(present, first_block, per_col, 0)
    weight_part, lower_part = assemble_every_factor((own_part, near_part, mask_part))
    weights, lower_factors = (
        lax.all_gather(weight_part, "col", axis=0, tiled=True),
        lax.all_gather(lower_part, "col", axis=0, tiled=True),
    )
    white_noise = normals.reshape(columns, resident_block_list, points)
    noise_portion = jnp.einsum(
        "rga,jra->jrg", lower_factors, white_noise, precision=lax.Precision.HIGHEST
    )
    values_now = jnp.zeros((columns, resident_block_list, points), jnp.float32)
    near_vals = jnp.zeros((columns, entries, points), jnp.float32)
    slot_range = jnp.arange(CAP, dtype=jnp.int32)
    for section_now in range(SECTIONS):
        updated = (
            jnp.einsum(
                "rga,jra->jrg",
                weights,
                near_vals.reshape(columns, resident_block_list, K * points),
                precision=lax.Precision.HIGHEST,
            )
            + noise_portion
        )
        values_now = jnp.where((sections == section_now)[None, :, None], updated, values_now)
        if section_now + 1 < SECTIONS:
            choose = (sections[None, :] == section_now) & (within[None, :] == slot_range[:, None])
            slot_block = jnp.sum(choose.astype(jnp.int32) * slot_ids[None, :], axis=1)
            filled = jnp.any(choose, axis=1).astype(jnp.float32)
            packed = jnp.take(values_now, slot_block, axis=1) * filled[None, :, None]
            gathered = lax.all_gather(packed, "blk", axis=1, tiled=True)
            fetched = jnp.take(gathered, slot_key, axis=1)
            near_vals = jnp.where((near_section == section_now)[None, :, None], fetched, near_vals)
    return values_now.reshape(columns, resident_block_list * points)


def solution(mesh):
    in_specs = (P("blk", None, None), P("blk", None), P("blk"), P("col", "blk"))
    out_specs = P("col", "blk")
    return jax.shard_map(local, mesh=mesh, in_specs=in_specs, out_specs=out_specs, check_vma=False)
```

profile of v0, /device:TPU:1, one launch (start us, length us, event | category | flops | bytes accessed | tf_op | source)
XLA Modules:
  0.0 839.3 jit_solution(6595695963177347756)
XLA Ops:
  12.0 58.5 %all-gather = s32[128,8,2]{1,2,0:T(2,128)S(1)} all-gather(s32[1,8,2]{1,2,0:T(2,128)S(1)} %add_bitcast_fusion), channel_id=1, replica_groups=mesh['blk'=128,'col'=4] {'blk'}, dimensions={0}, use_global_device_ids=true | all-gather | bytes 8256 | tf_op jit(solution)/shard_map/all_gather | solution.py:53
  71.2 24.4 %all-gather.4.cloned.1.call-done = f32[1024,2,128]{2,1,0:T(2,128)} async-done(((f32[8,2,128]{2,1,0:T(2,128)}), f32[1024,2,128]{2,1,0:T(2,128)}) %all-gather.4.cloned.1.call-update) | async-done | bytes 1048592 | tf_op jit(solution)/shard_map/all_gather | solution.py:52
  97.8 330.6 %while.15 = (s32[]{:T(128)}, f32[2,128,512]{2,1,0:T(8,128)S(1)}, f32[2,128,128]{2,1,0:T(8,128)S(1)}, f32[2,2,512]{2,0,1:T(2,128)S(1)}, f32[2,512]{1,0:T(2,128)S(...) while((s32[]{:T(128)}, f32[2,128,512]{2,1,0:T(8,128)S(1)}, ...), condition=%wide.region_13.14_spmd, body=%wide.region_2.13_spmd.sunk | while | flops 1016400000 | bytes 14919042 | solution.py:37
  122.5 11.7 %cholesky.533 = f32[128,128]{1,0:T(8,128)S(1)} custom-call(f32[128,128]{1,0:T(8,128)S(1)} %cholesky.532), custom_call_target="Cholesky" | custom-call | tf_op jit(solution)/shard_map/while/body/eval_jaxpr/jit(cholesky)/cholesky | solution.py:27
  144.9 11.7 %cholesky.536 = f32[128,128]{1,0:T(8,128)S(1)} custom-call(f32[128,128]{1,0:T(8,128)S(1)} %cholesky.535), custom_call_target="Cholesky" | custom-call | tf_op jit(solution)/shard_map/while/body/eval_jaxpr/jit(cholesky)/cholesky | solution.py:27
  169.0 11.7 %cholesky.538 = f32[128,128]{1,0:T(8,128)S(1)} custom-call(f32[128,128]{1,0:T(8,128)S(1)} %cholesky.537), custom_call_target="Cholesky" | custom-call | tf_op jit(solution)/shard_map/while/body/eval_jaxpr/jit(cholesky)/cholesky | solution.py:27
  192.3 11.7 %cholesky.539 = f32[128,128]{1,0:T(8,128)S(1)} custom-call(f32[128,128]{1,0:T(8,128)S(1)} %convolution_subtract_fusion.20), custom_call_target="Cholesky" | custom-call | tf_op jit(solution)/shard_map/while/body/eval_jaxpr/jit(cholesky)/cholesky | solution.py:27
  213.1 39.3 %custom-call.75 = f32[4,128,128]{1,2,0:T(8,128)S(1)} custom-call(f32[4,128,128]{2,1,0:T(8,128)S(1)} %get-tuple-element.247), custom_call_target="InvertDiagBlocksLowerTriangular" | custom-call | tf_op jit(solution)/shard_map/while/body/eval_jaxpr/triangular_solve | solution.py:30
  255.6 11.7 %cholesky.543 = f32[128,128]{1,0:T(8,128)S(1)} custom-call(f32[128,128]{1,0:T(8,128)S(1)} %fusion.204), custom_call_target="Cholesky" | custom-call | tf_op jit(solution)/shard_map/while/body/eval_jaxpr/jit(cholesky)/cholesky | solution.py:33
  272.4 11.7 %cholesky.533 = f32[128,128]{1,0:T(8,128)S(1)} custom-call(f32[128,128]{1,0:T(8,128)S(1)} %cholesky.532), custom_call_target="Cholesky" | custom-call | tf_op jit(solution)/shard_map/while/body/eval_jaxpr/jit(cholesky)/cholesky | solution.py:27
  294.8 11.7 %cholesky.536 = f32[128,128]{1,0:T(8,128)S(1)} custom-call(f32[128,128]{1,0:T(8,128)S(1)} %cholesky.535), custom_call_target="Cholesky" | custom-call | tf_op jit(solution)/shard_map/while/body/eval_jaxpr/jit(cholesky)/cholesky | solution.py:27
  318.9 11.7 %cholesky.538 = f32[128,128]{1,0:T(8,128)S(1)} custom-call(f32[128,128]{1,0:T(8,128)S(1)} %cholesky.537), custom_call_target="Cholesky" | custom-call | tf_op jit(solution)/shard_map/while/body/eval_jaxpr/jit(cholesky)/cholesky | solution.py:27
  342.2 11.7 %cholesky.539 = f32[128,128]{1,0:T(8,128)S(1)} custom-call(f32[128,128]{1,0:T(8,128)S(1)} %convolution_subtract_fusion.20), custom_call_target="Cholesky" | custom-call | tf_op jit(solution)/shard_map/while/body/eval_jaxpr/jit(cholesky)/cholesky | solution.py:27
  363.1 39.3 %custom-call.75 = f32[4,128,128]{1,2,0:T(8,128)S(1)} custom-call(f32[4,128,128]{2,1,0:T(8,128)S(1)} %get-tuple-element.247), custom_call_target="InvertDiagBlocksLowerTriangular" | custom-call | tf_op jit(solution)/shard_map/while/body/eval_jaxpr/triangular_solve | solution.py:30
  405.5 11.7 %cholesky.543 = f32[128,128]{1,0:T(8,128)S(1)} custom-call(f32[128,128]{1,0:T(8,128)S(1)} %fusion.204), custom_call_target="Cholesky" | custom-call | tf_op jit(solution)/shard_map/while/body/eval_jaxpr/jit(cholesky)/cholesky | solution.py:33
  429.5 11.0 %all_gather.36 = f32[8,128,128]{2,1,0:T(8,128)S(1)} all-gather(f32[2,128,128]{2,1,0:T(8,128)S(1)} %get-tuple-element.41), channel_id=1, replica_groups=mesh['blk'=128,'col'=4] {'col'}, dimensions={0}, use_global_device_ids=true | all-gather | bytes 655360 | tf_op jit(solution)/shard_map/all_gather | solution.py:82
  441.4 19.4 %all-gather.6.cloned.1.call-done = f32[8,128,512]{2,1,0:T(8,128)} async-done(((f32[2,128,512]{2,1,0:T(8,128)}), f32[8,128,512]{2,1,0:T(8,128)}) %all-gather.6.cloned.1.call-update) | async-done | bytes 2097168 | tf_op jit(solution)/shard_map/all_gather | solution.py:81
  464.9 52.5 %all_gather.37 = f32[4,256,128]{2,0,1:T(4,128)S(1)} all-gather(f32[4,2,128]{2,0,1:T(4,128)S(1)} %bitcast_multiply_fusion.6), channel_id=1, replica_groups=mesh['blk'=128,'col'=4] {'blk'}, dimensions={1}, use_global_device_ids=true | all-gather | bytes 528384 | tf_op jit(solution)/shard_map/all_gather | solution.py:107
  520.7 48.8 %all_gather.38 = f32[4,256,128]{2,0,1:T(4,128)S(1)} all-gather(f32[4,2,128]{2,0,1:T(4,128)S(1)} %bitcast_multiply_fusion.5), channel_id=1, replica_groups=mesh['blk'=128,'col'=4] {'blk'}, dimensions={1}, use_global_device_ids=true | all-gather | bytes 528384 | tf_op jit(solution)/shard_map/all_gather | solution.py:107
  572.7 48.6 %all_gather.39 = f32[4,256,128]{2,0,1:T(4,128)S(1)} all-gather(f32[4,2,128]{2,0,1:T(4,128)S(1)} %bitcast_multiply_fusion.4), channel_id=1, replica_groups=mesh['blk'=128,'col'=4] {'blk'}, dimensions={1}, use_global_device_ids=true | all-gather | bytes 528384 | tf_op jit(solution)/shard_map/all_gather | solution.py:107
  624.6 48.8 %all_gather.40 = f32[4,256,128]{2,0,1:T(4,128)S(1)} all-gather(f32[4,2,128]{2,0,1:T(4,128)S(1)} %bitcast_multiply_fusion.3), channel_id=1, replica_groups=mesh['blk'=128,'col'=4] {'blk'}, dimensions={1}, use_global_device_ids=true | all-gather | bytes 528384 | tf_op jit(solution)/shard_map/all_gather | solution.py:107
  676.6 48.4 %all_gather.41 = f32[4,256,128]{2,0,1:T(4,128)S(1)} all-gather(f32[4,2,128]{2,0,1:T(4,128)S(1)} %bitcast_multiply_fusion.2), channel_id=1, replica_groups=mesh['blk'=128,'col'=4] {'blk'}, dimensions={1}, use_global_device_ids=true | all-gather | bytes 528384 | tf_op jit(solution)/shard_map/all_gather | solution.py:107
  728.3 49.0 %all_gather.42 = f32[4,256,128]{2,0,1:T(4,128)S(1)} all-gather(f32[4,2,128]{2,0,1:T(4,128)S(1)} %bitcast_multiply_fusion.1), channel_id=1, replica_groups=mesh['blk'=128,'col'=4] {'blk'}, dimensions={1}, use_global_device_ids=true | all-gather | bytes 528384 | tf_op jit(solution)/shard_map/all_gather | solution.py:107
  780.5 48.4 %all_gather.43 = f32[4,256,128]{2,0,1:T(4,128)S(1)} all-gather(f32[4,2,128]{2,0,1:T(4,128)S(1)} %bitcast_multiply_fusion), channel_id=1, replica_groups=mesh['blk'=128,'col'=4] {'blk'}, dimensions={1}, use_global_device_ids=true | all-gather | bytes 528384 | tf_op jit(solution)/shard_map/all_gather | solution.py:107
  (235 shorter events, 150.9 us)
Async XLA Ops:
  6.5 433.9 %copy-start = (f32[4,1024]{1,0:T(4,128)S(1)}, f32[4,1024]{1,0:T(4,128)}, u32[]{:S(2)}) copy-start(f32[4,1024]{1,0:T(4,128)} %param.13) | copy-start | bytes 49156
  6.5 90.5 %copy-start.3 = (s32[8,4]{0,1:T(4,128)S(1)}, s32[8,4]{0,1:T(4,128)}, u32[]{:S(2)}) copy-start(s32[8,4]{0,1:T(4,128)} %param.11) | copy-start | bytes 388
  6.5 89.0 %all-gather.4.cloned.1.call-start = ((), (), s32[]{:S(2)}) async-start(), calls=%async_computation | async-start | bytes 1056768 | tf_op jit(solution)/shard_map/all_gather | solution.py:52
  7.3 453.5 %all-gather.6.cloned.1.call-start = ((), (), s32[]{:S(2)}) async-start(), calls=%async_computation.1 | async-start | bytes 2621440 | tf_op jit(solution)/shard_map/all_gather | solution.py:81
  428.4 0.8 copy-start.2
  460.7 57.4 %copy-start.1 = (f32[8,128,512]{2,1,0:T(8,128)S(1)}, f32[8,128,512]{2,1,0:T(8,128)}, u32[]{:S(2)}) copy-start(f32[8,128,512]{2,1,0:T(8,128)} %all-gather.6.cloned.1.call-done) | copy-start | bytes 6291460
Sparse Core Ops, SparseCore 0:
  10.4 85.1 all-gather.3
  429.3 31.3 all-gather.5
where the time goes:
time: 842 us; the launch traced here: 839 us
  blocking collectives  414 us (49%)
  other arithmetic  271 us (32%)
  waiting for transfers between devices  44.5 us (5%)
  loops' own time  36.3 us (4%)
  matrix products  31.3 us (4%)
  local copies, waits for them, and re-layouts  28.4 us (3%)
  between operations  14 us (2%)
    all_gather x7, blocking collectives, local(): gathered = lax.all_gather(packed, 'blk', axis=1, tiled=True)  345 us
    another operation x28, other arithmetic, factor(): chol_near = jnp.linalg.cholesky(near_cov)  157 us
    another operation x6, other arithmetic, factor(): lax.linalg.triangular_solve(chol_near, whitened, left_side=True, lower=Tr...  78.9 us
    all_gather x1, blocking collectives, local(): part_info = lax.all_gather(section_rank, 'blk', axis=0, tiled=True)  58.5 us
    another operation x1, loops' own time, assemble_every_factor(): lax.map(lambda triple: factor(triple[0], triple[1], triple[2]), inputs)  36.1 us
    another operation x6, other arithmetic, factor(): return (weight_t.T, jnp.linalg.cholesky(cond_cov))  24.9 us
    all_gather x1, waiting for transfers between devices, local(): part_coords = lax.all_gather(coords, 'blk', axis=0, tiled=True)  24.4 us
    all_gather x1, waiting for transfers between devices, local(): lax.all_gather(weight_part, 'col', axis=0, tiled=True)  19.4 us
  transfers between devices with their start and end apart: 2, of which 2 were waited for; matrix products, arithmetic and copies ran while one was open for 1% of the time, Pallas kernels for 0%

commit v1 on v0

v1 whole, which is shorter than its diff:
```python
import jax
import jax.numpy as jnp
from jax import lax
from jax.experimental import pallas as pl
from jax.experimental.pallas import tpu as pltpu
from jax.sharding import PartitionSpec as P

K = 4
SECTIONS = 8
CAP = 2
B = 128
ROUNDS = SECTIONS - 1
LINE = 8
ZERO_TILE = ROUNDS * 2 * LINE * CAP

length_scale = 0.5
nugget_var = 0.1

HIGHEST = lax.Precision.HIGHEST
F32 = jnp.float32
BF16 = jnp.bfloat16


def iota(shape, dim):
    return lax.broadcasted_iota(jnp.int32, shape, dim)


def place():
    blk = lax.axis_index("blk")
    core = blk % 2
    y = (blk // 2) % LINE
    z = blk // (2 * LINE)
    along = (1 - core) * z + core * y
    across = (1 - core) * y + core * z
    return core, along, across


def device_at(core, along, across, other_core):
    chip = (1 - core) * (along * LINE + across) + core * (across * LINE + along)
    return chip * 2 + other_core


def line_targets(core, along, across):
    same = [
        (device_at(core, (along + d) % LINE, across, core), 2 * along + core) for d in range(1, LINE)
    ]
    other = [
        (device_at(core, along, (across + d) % LINE, 1 - core), 2 * across + core) for d in range(LINE)
    ]
    return same + other


def line_sources(core, along, across):
    same = [device_at(core, (along + d) % LINE, across, core) for d in range(1, LINE)]
    other = [device_at(core, (along + d) % LINE, across, 1 - core) for d in range(LINE)]
    return same + other


def cross_peers(core, along, across):
    return [
        (device_at(core, along, (across + d) % LINE, core), (across + d) % LINE) for d in range(1, LINE)
    ]


def greet(core, along, across):
    barrier = pltpu.get_barrier_semaphore()
    col = lax.axis_index("col")
    cols = lax.axis_size("col")
    count = 0
    for device in line_sources(core, along, across):
        pl.semaphore_signal(barrier, inc=1, device_id={"blk": device}, device_id_type=pl.DeviceIdType.MESH)
        count += 1
    for device, _ in cross_peers(core, along, across):
        pl.semaphore_signal(barrier, inc=1, device_id={"blk": device}, device_id_type=pl.DeviceIdType.MESH)
        count += 1
    for d in range(1, cols):
        pl.semaphore_signal(
            barrier, inc=1, device_id={"col": (col + d) % cols}, device_id_type=pl.DeviceIdType.MESH
        )
        count += 1
    pl.semaphore_wait(barrier, count)


def remote(src, dst, send_sem, recv_sem, device_id):
    return pltpu.make_async_remote_copy(
        src_ref=src,
        dst_ref=dst,
        send_sem=send_sem,
        recv_sem=recv_sem,
        device_id=device_id,
        device_id_type=pl.DeviceIdType.MESH,
    )


def wait_bytes(ref, sem):
    pltpu.make_async_copy(ref, ref, sem).wait()


def exchange_kernel(
    slot_ref,
    coords_ref,
    code_ref,
    ids_ref,
    asked_ref,
    normals_ref,
    near_ref,
    key_ref,
    draws_ref,
    own_a,
    own_b,
    own_n,
    got_a,
    got_b,
    got_n,
    picked,
    got_p,
    send_sems,
    recv_sems,
):
    core, along, across = place()
    col = lax.axis_index("col")
    cols = lax.axis_size("col")
    my_slot = 2 * along + core
    own_a[0] = coords_ref[:, 0, :]
    own_a[1] = coords_ref[:, 1, :]
    own_a[2] = code_ref[...]
    own_b[0] = ids_ref[...]
    own_b[1] = asked_ref[...]
    for owner in range(cols):
        for half in range(2):
            slot = slot_ref[owner + half * cols]
            drawn = jnp.zeros((4, B), F32)
            for at in range(LINE):
                drawn = drawn + normals_ref[:, at * B : (at + 1) * B] * (slot == at).astype(F32)
            own_n[owner, half * 4 : half * 4 + 4, :] = drawn
    greet(core, along, across)
    for device, slot in line_targets(core, along, across):
        remote(own_a, got_a.at[slot], send_sems.at[0], recv_sems.at[0], {"blk": device}).start()
    for device, _ in cross_peers(core, along, across):
        remote(own_b, got_b.at[across], send_sems.at[1], recv_sems.at[1], {"blk": device}).start()
    for d in range(1, cols):
        to = (col + d) % cols
        remote(own_n.at[to], got_n.at[col], send_sems.at[2], recv_sems.at[2], {"col": to}).start()
    got_a[my_slot] = own_a[...]
    got_b[across] = own_b[...]
    got_n[col] = own_n[col]
    lane = iota((1, B), 1)
    lane_dev = device_at(core, lane // (2 * LINE), across, (lane // LINE) % 2)
    lane_block = lane_dev * LINE + lane % LINE
    sub = iota((LINE, B), 0)
    entry_half = (iota((1, B), 1) // K) % 2
    wait_bytes(got_a.at[pl.ds(0, 2 * LINE - 1)], recv_sems.at[0])
    wait_bytes(got_b.at[pl.ds(0, LINE - 1)], recv_sems.at[1])
    chosen = jnp.concatenate(
        [(got_b[peer, 0] == lane_block).astype(F32) for peer in range(LINE)], axis=0
    )
    for axis in range(2):
        held = got_a[:, axis].reshape(B, B)
        moved = jnp.dot(chosen, held, precision=HIGHEST, preferred_element_type=F32)
        picked[:, axis] = moved.reshape(LINE, LINE, B)
    for device, peer in cross_peers(core, along, across):
        remote(picked.at[peer], got_p.at[across], send_sems.at[3], recv_sems.at[3], {"blk": device}).start()
    got_p[across] = picked[across]
    sums = [jnp.zeros((LINE, B), jnp.int32) for _ in range(LINE)]
    for dev in range(2 * LINE):
        block = device_at(core, dev // 2, across, dev % 2) * LINE + sub
        value = got_a[dev, 2].astype(jnp.int32) + (2 * dev + 1)
        for peer in range(LINE):
            sums[peer] = sums[peer] + jnp.where(block == got_b[peer, 1], value, 0)
    for peer in range(LINE):
        total = jnp.sum(sums[peer], axis=0, keepdims=True)
        value = total - 1
        turned = value + entry_half * (1 - 2 * (value % 2))
        key_ref[peer : peer + 1, :] = jnp.where(total > 0, turned, ZERO_TILE)
    wait_bytes(got_n.at[pl.ds(0, cols - 1)], recv_sems.at[2])
    draws_ref[...] = got_n[...]
    wait_bytes(got_p.at[pl.ds(0, LINE - 1)], recv_sems.at[3])
    for axis in range(2):
        near = got_p[0, axis]
        for peer in range(1, LINE):
            near = near + got_p[peer, axis]
        near_ref[axis] = near
    wait_bytes(got_a.at[pl.ds(0, 2 * LINE - 1)], send_sems.at[0])
    wait_bytes(got_b.at[pl.ds(0, LINE - 1)], send_sems.at[1])
    wait_bytes(got_n.at[pl.ds(0, cols - 1)], send_sems.at[2])
    wait_bytes(got_p.at[pl.ds(0, LINE - 1)], send_sems.at[3])


def split3(x):
    high = x.astype(BF16).astype(F32)
    rest = x - high
    middle = rest.astype(BF16).astype(F32)
    return high, middle, rest - middle


def thin_product(left, right):
    l1, l2, l3 = split3(left)
    r1, r2, r3 = split3(right)
    tall_left = jnp.concatenate([l1, l1, l2, l2, l1, l3], axis=0).astype(BF16)
    tall_right = jnp.concatenate([r1, r2, r1, r2, r3, r1], axis=0).astype(BF16)
    return lax.dot_general(tall_left, tall_right, (((0,), (0,)), ((), ())), preferred_element_type=F32)


def spread(tile, first):
    return [jnp.broadcast_to(tile[:, first + j : first + j + 1], (8, B)) for j in range(8)]


def weighted_rows(factors, rows):
    terms = [factors[j] * rows[j : j + 1, :] for j in range(8)]
    return ((terms[0] + terms[1]) + (terms[2] + terms[3])) + ((terms[4] + terms[5]) + (terms[6] + terms[7]))


def eliminate(rows, columns, sub):
    columns = list(columns)
    full = rows
    scales = []
    for j in range(8):
        below, here = sub > j, sub == j
        pivot = columns[j][j : j + 1, :]
        inverse = 1.0 / pivot
        factors = columns[j] * inverse
        under = jnp.where(below, factors, 0.0)
        scaled = full[j : j + 1, :] * inverse
        full = jnp.where(here, scaled, full - columns[j] * scaled)
        rows = rows - under * rows[j : j + 1, :]
        for later in range(j + 1, 8):
            columns[later] = jnp.where(
                here, columns[later] * inverse, columns[later] - factors * columns[later][j : j + 1, :]
            )
        scales.append(lax.rsqrt(pivot))
    scale = scales[7]
    for j in range(7):
        scale = jnp.where(sub == j, scales[j], scale)
    return rows * scale, full


def inverse_factors(matrices):
    sub, lane = iota((8, B), 0), iota((8, B), 1)
    wide = iota((B, B), 1)
    matrices = list(matrices)
    ahead = [m[0:8] for m in matrices]
    panels = [[] for _ in matrices]
    for panel in range(B // 8):
        at = 8 * panel
        inside = (lane >= at) & (lane < at + 8)
        for q in range(len(matrices)):
            unit = jnp.where(lane == sub + at, 1.0, 0.0)
            done, full = eliminate(jnp.where(inside, unit, ahead[q]), spread(ahead[q], at), sub)
            panels[q].append(jnp.where(lane < at + 8, done, 0.0))
            if at + 8 < B:
                following = matrices[q][at + 8 : at + 16]
                ahead[q] = jnp.where(inside, 0.0, following) - weighted_rows(spread(following, at), full)
                kept = jnp.where((wide >= at) & (wide < at + 8), 0.0, matrices[q])
                matrices[q] = kept - thin_product(done, done)
    return [jnp.concatenate(p, axis=0) for p in panels]


def factor_rows(rows, columns, sub):
    columns = list(columns)
    scales = []
    for j in range(8):
        below = sub > j
        pivot = columns[j][j : j + 1, :]
        inverse = 1.0 / pivot
        factors = jnp.where(below, columns[j] * inverse, 0.0)
        rows = rows - factors * rows[j : j + 1, :]
        for later in range(j + 1, 8):
            columns[later] = columns[later] - factors * columns[later][j : j + 1, :]
        scales.append(lax.rsqrt(pivot))
    scale = scales[7]
    for j in range(7):
        scale = jnp.where(sub == j, scales[j], scale)
    return rows * scale


def upper_cholesky(matrices):
    sub, lane = iota((8, B), 0), iota((8, B), 1)
    matrices = list(matrices)
    ahead = [m[0:8] for m in matrices]
    panels = [[] for _ in matrices]
    for panel in range(B // 8):
        at = 8 * panel
        for q in range(len(matrices)):
            rows = ahead[q]
            done = factor_rows(rows, spread(rows, at), sub)
            done = jnp.where(lane >= sub + at, done, 0.0)
            panels[q].append(done)
            if at + 8 < B:
                following = matrices[q][at + 8 : at + 16]
                turned = done[:, at + 8 : at + 16].T
                factors = [jnp.broadcast_to(turned[:, j : j + 1], (8, B)) for j in range(8)]
                ahead[q] = following - weighted_rows(factors, done)
                matrices[q] = matrices[q] - thin_product(done, done)
    return [jnp.concatenate(p, axis=0) for p in panels]


def multiply(left, right):
    return jnp.dot(left, right, precision=HIGHEST, preferred_element_type=F32)


def multiply_tn(left, right):
    return lax.dot_general(
        left, right, (((0,), (0,)), ((), ())), precision=HIGHEST, preferred_element_type=F32
    )


def covariance(row_x, row_y, col_x, col_y):
    dx = col_x - row_x
    dy = col_y - row_y
    return jnp.exp(-jnp.sqrt(dx * dx + dy * dy) / length_scale)


def factor_kernel(slot_ref, there_ref, coords_ref, near_ref, draws_ref, weight_ref, noise_ref, cov, inverses):
    eye = (iota((B, B), 0) == iota((B, B), 1)).astype(F32)
    for q in range(2):
        own = coords_ref[slot_ref[q]]
        points = [
            (near_ref[0, q * K + k : q * K + k + 1, :], near_ref[1, q * K + k : q * K + k + 1, :])
            for k in range(K)
        ] + [(own[0:1], own[1:2])]
        there = [there_ref[q * K + k].astype(F32) for k in range(K)] + [jnp.float32(1.0)]
        for a in range(K + 1):
            col_x = jnp.broadcast_to(points[a][0], (B, B)).T
            col_y = jnp.broadcast_to(points[a][1], (B, B)).T
            for b in range(a, K + 1):
                block = covariance(points[b][0], points[b][1], col_x, col_y) * (there[a] * there[b])
                if a == b:
                    block = block + (nugget_var * there[a] + (1.0 - there[a])) * eye
                cov[q, a, :, b * B : (b + 1) * B] = block

    def step(k, carry):
        start = pl.multiple_of(k * B, B)
        inverse = inverse_factors([cov[q, k, :, pl.ds(start, B)] for q in range(2)])
        for q in range(2):
            inverses[q, k] = inverse[q]
        for at in range(K):

            @pl.when(k == at)
            def _(at=at):
                for q in range(2):
                    rest = slice((at + 1) * B, (K + 1) * B)
                    white = multiply(inverse[q], cov[q, at, :, rest])
                    cov[q, at, :, rest] = white
                    for row in range(at + 1, K + 1):
                        first = (row - at - 1) * B
                        cov[q, row, :, row * B :] = cov[q, row, :, row * B :] - multiply_tn(
                            white[:, first : first + B], white[:, first:]
                        )

        return carry

    lax.fori_loop(0, K, step, 0)
    for q in range(2):
        for k in reversed(range(K)):
            total = cov[q, k, :, K * B :]
            if k + 1 < K:
                total = total - multiply(cov[q, k, :, (k + 1) * B : K * B], weight_ref[q, (k + 1) * B :, :])
            weight_ref[q, k * B : (k + 1) * B, :] = multiply_tn(inverses[q, k], total)
    upper = upper_cholesky([cov[q, K, :, K * B :] for q in range(2)])
    rows = draws_ref.shape[0] * draws_ref.shape[1]
    noise = jnp.dot(
        draws_ref[...].reshape(rows, B),
        jnp.concatenate(upper, axis=1),
        precision=HIGHEST,
        preferred_element_type=F32,
    )
    half = (iota((rows, B), 0) // 4) % 2
    noise_ref[...] = jnp.where(half == 0, noise[:, :B], noise[:, B:]).reshape(noise_ref.shape)


def section_kernel(
    key_ref,
    rank_ref,
    out_key_ref,
    weight_ref,
    noise_ref,
    out_ref,
    early,
    late,
    got_noise,
    values,
    turned,
    got_line,
    held,
    picked,
    got_cross,
    high,
    low,
    local_sem,
    wave_send,
    wave_recv,
    line_send,
    line_recv,
    cross_send,
    cross_recv,
):
    core, along, across = place()
    col = lax.axis_index("col")
    cols = lax.axis_size("col")
    my_slot = 2 * along + core
    sub = iota((8, B), 0)
    held[ZERO_TILE] = jnp.zeros((8, B), F32)
    greet(core, along, across)
    peers = [(col + d) % cols for d in range(1, cols)]
    for to in peers:
        remote(noise_ref.at[to], got_noise.at[col], wave_send.at[0], wave_recv.at[0], {"col": to}).start()
    for wave, buffer in ((0, early), (1, late)):
        for to in peers:
            remote(
                weight_ref.at[wave], buffer.at[col], wave_send.at[1 + wave], wave_recv.at[1 + wave], {"col": to}
            ).start()
        pltpu.make_async_copy(weight_ref.at[wave], buffer.at[col], local_sem.at[wave]).start()
    got_noise[col] = noise_ref[col]

    def noise_of(section):
        tiles = []
        for slot in range(CAP):
            rank = rank_ref[CAP * section + slot]
            tile = got_noise[rank % cols]
            swapped = pltpu.roll(tile, 4, 0)
            keep = (rank // cols == slot).astype(F32)
            tiles.append(tile * keep + swapped * (1.0 - keep))
        return jnp.where(sub < 4, tiles[0], tiles[1])

    def spread_values(s, tile):
        values[s] = tile
        turned[CAP * s] = tile
        turned[CAP * s + 1] = pltpu.roll(tile, 4, 0)

    def prepare(section, both):
        for slot in range(CAP):
            rank = rank_ref[CAP * section + slot]
            place_in_wave = rank % cols
            weight = early[place_in_wave]
            if both:
                is_late = (rank // cols).astype(F32)
                weight = weight * (1.0 - is_late) + late[place_in_wave] * is_late
            part = weight.astype(BF16)
            high[:, slot * B : (slot + 1) * B] = part
            low[:, slot * B : (slot + 1) * B] = (weight - part.astype(F32)).astype(BF16)

    def share(s):
        for device, slot in line_targets(core, along, across):
            remote(
                values.at[s], got_line.at[s, slot], line_send.at[s], line_recv.at[s], {"blk": device}
            ).start()
        got_line[s, my_slot] = values[s]

    def pass_on(s):
        wait_bytes(got_line.at[s, pl.ds(0, 2 * LINE - 1)], line_recv.at[s])
        first = s * (2 * LINE * CAP)
        for dev in range(2 * LINE):
            tile = got_line[s, dev]
            held[first + 2 * dev] = tile
            held[first + 2 * dev + 1] = pltpu.roll(tile, 4, 0)

        def pick(peer, slot_there):
            lanes = (s + 1) * (CAP * K)
            for k in range(K):
                upper = held[key_ref[peer, lanes + k]]
                lower = held[key_ref[peer, lanes + K + k]]
                slot_there[k] = jnp.where(sub < 4, upper, lower)

        for device, peer in cross_peers(core, along, across):
            pick(peer, picked.at[s, peer])
            remote(
                picked.at[s, peer], got_cross.at[s, across], cross_send.at[s], cross_recv.at[s], {"blk": device}
            ).start()
        pick(across, got_cross.at[s, across])

    def collect(s):
        wait_bytes(got_cross.at[s, pl.ds(0, LINE - 1)], cross_recv.at[s])
        near = []
        for k in range(K):
            tile = got_cross[s, 0, k]
            for peer in range(1, LINE):
                tile = tile + got_cross[s, peer, k]
            near.append(tile)
        near = jnp.concatenate(near, axis=1)
        part = near.astype(BF16).astype(F32)
        both = jnp.concatenate([part, near - part], axis=0).astype(BF16)
        first = jnp.dot(both, high[...], preferred_element_type=F32)
        second = jnp.dot(both[0:8], low[...], preferred_element_type=F32)
        total = first[0:8] + (first[8:16] + second)
        update = jnp.where(sub < 4, total[:, :B], total[:, B:])
        spread_values(s + 1, update + noise_of(s + 1))

    wait_bytes(got_noise.at[pl.ds(0, cols - 1)], wave_recv.at[0])
    spread_values(0, noise_of(0))
    share(0)
    pass_on(0)
    wait_bytes(early.at[pl.ds(0, cols - 1)], wave_recv.at[1])
    pltpu.make_async_copy(weight_ref.at[0], early.at[col], local_sem.at[0]).wait()
    prepare(1, False)
    collect(0)
    share(1)
    wait_bytes(late.at[pl.ds(0, cols - 1)], wave_recv.at[2])
    pltpu.make_async_copy(weight_ref.at[1], late.at[col], local_sem.at[1]).wait()

    def section(s, carry):
        prepare(s + 1, True)
        pass_on(s)
        collect(s)

        @pl.when(s + 1 < ROUNDS)
        def _():
            share(s + 1)

        return carry

    lax.fori_loop(1, ROUNDS, section, 0)
    for block in range(out_ref.shape[1] // B):
        out_ref[:, block * B : (block + 1) * B] = turned[out_key_ref[block]][0:4]
    wait_bytes(got_noise.at[pl.ds(0, cols - 1)], wave_send.at[0])
    wait_bytes(early.at[pl.ds(0, cols - 1)], wave_send.at[1])
    wait_bytes(late.at[pl.ds(0, cols - 1)], wave_send.at[2])

    def finish(s, carry):
        wait_bytes(got_line.at[s, pl.ds(0, 2 * LINE - 1)], line_send.at[s])
        wait_bytes(got_cross.at[s, pl.ds(0, LINE - 1)], cross_send.at[s])
        return carry

    lax.fori_loop(0, ROUNDS, finish, 0)


VMEM_SPEC = pl.BlockSpec(memory_space=pltpu.VMEM)
SMEM_SPEC = pl.BlockSpec(memory_space=pltpu.SMEM)
FACTOR_SCRATCH = [pltpu.VMEM((2, K + 1, B, (K + 1) * B), F32), pltpu.VMEM((2, K, B, B), F32)]
VMEM_LIMIT = 40 * 1024 * 1024


def local(coords, neighbours, sections, normals):
    blocks = coords.shape[0]
    cols = lax.axis_size("col")
    col = lax.axis_index("col")
    i32 = jnp.int32
    slots = jnp.arange(blocks, dtype=i32)
    same = sections[None, :] == sections[:, None]
    lower = sections[None, :] < sections[:, None]
    earlier = slots[None, :] < slots[:, None]
    within = jnp.sum((same & earlier).astype(i32), axis=1)
    rank = jnp.sum((lower | (same & earlier)).astype(i32), axis=1)
    by_rank = rank[None, :] == slots[:, None]
    slot_of_rank = jnp.sum(by_rank.astype(i32) * slots[None, :], axis=1)
    cells = jnp.arange(SECTIONS * CAP, dtype=i32)
    in_cell = cells[:, None] == (sections * CAP + within)[None, :]
    rank_of_cell = jnp.sum(in_cell.astype(i32) * rank[None, :], axis=1)
    listed = neighbours + 1
    asked = jnp.sum(in_cell.astype(i32)[:, :, None] * listed[None, :, :], axis=1).reshape(-1) - 1
    asked = jnp.pad(asked, (0, B - asked.shape[0]), constant_values=-1)
    mine = jnp.stack([col, col + cols])
    is_mine = rank[None, :] == mine[:, None]
    my_slots = jnp.sum(is_mine.astype(i32) * slots[None, :], axis=1)
    ids = jnp.sum(is_mine.astype(i32)[:, :, None] * listed[None, :, :], axis=1).reshape(-1) - 1
    there = (ids >= 0).astype(i32)
    code = (sections * (2 * LINE * CAP) + within).astype(F32)
    out_key = sections * CAP + within

    def tile(v):
        return jnp.broadcast_to(v[:, None], (blocks, B))

    shape = jax.ShapeDtypeStruct
    near, key, draws = pl.pallas_call(
        exchange_kernel,
        out_shape=(shape((2, 8, B), F32), shape((LINE, B), i32), shape((cols, 8, B), F32)),
        in_specs=[SMEM_SPEC] + [VMEM_SPEC] * 5,
        out_specs=(VMEM_SPEC,) * 3,
        scratch_shapes=[
            pltpu.VMEM((3, 8, B), F32),
            pltpu.VMEM((2, 8, B), i32),
            pltpu.VMEM((cols, 8, B), F32),
            pltpu.VMEM((2 * LINE, 3, 8, B), F32),
            pltpu.VMEM((LINE, 2, 8, B), i32),
            pltpu.VMEM((cols, 8, B), F32),
            pltpu.VMEM((LINE, 2, 8, B), F32),
            pltpu.VMEM((LINE, 2, 8, B), F32),
            pltpu.SemaphoreType.DMA((4,)),
            pltpu.SemaphoreType.DMA((4,)),
        ],
        compiler_params=pltpu.CompilerParams(
            collective_id=0, has_side_effects=True, vmem_limit_bytes=VMEM_LIMIT
        ),
        name="exchange",
    )(slot_of_rank, coords, tile(code), tile(ids), jnp.broadcast_to(asked[None, :], (8, B)), normals)

    weight, noise = pl.pallas_call(
        factor_kernel,
        out_shape=(shape((2, K * B, B), F32), shape((cols, 8, B), F32)),
        in_specs=[SMEM_SPEC] * 2 + [VMEM_SPEC] * 3,
        out_specs=(VMEM_SPEC,) * 2,
        scratch_shapes=FACTOR_SCRATCH,
        compiler_params=pltpu.CompilerParams(vmem_limit_bytes=VMEM_LIMIT),
        name="factor",
    )(my_slots, there, coords, near, draws)

    return pl.pallas_call(
        section_kernel,
        out_shape=shape(normals.shape, F32),
        in_specs=[SMEM_SPEC] * 3 + [VMEM_SPEC] * 2,
        out_specs=VMEM_SPEC,
        scratch_shapes=[
            pltpu.VMEM((cols, K * B, B), F32),
            pltpu.VMEM((cols, K * B, B), F32),
            pltpu.VMEM((cols, 8, B), F32),
            pltpu.VMEM((SECTIONS, 8, B), F32),
            pltpu.VMEM((SECTIONS * CAP, 8, B), F32),
            pltpu.VMEM((ROUNDS, 2 * LINE, 8, B), F32),
            pltpu.VMEM((ZERO_TILE + 1, 8, B), F32),
            pltpu.VMEM((ROUNDS, LINE, K, 8, B), F32),
            pltpu.VMEM((ROUNDS, LINE, K, 8, B), F32),
            pltpu.VMEM((K * B, CAP * B), BF16),
            pltpu.VMEM((K * B, CAP * B), BF16),
            pltpu.SemaphoreType.DMA((2,)),
            pltpu.SemaphoreType.DMA((3,)),
            pltpu.SemaphoreType.DMA((3,)),
            pltpu.SemaphoreType.DMA((ROUNDS,)),
            pltpu.SemaphoreType.DMA((ROUNDS,)),
            pltpu.SemaphoreType.DMA((ROUNDS,)),
            pltpu.SemaphoreType.DMA((ROUNDS,)),
        ],
        compiler_params=pltpu.CompilerParams(
            collective_id=1, has_side_effects=True, vmem_limit_bytes=VMEM_LIMIT
        ),
        name="sections",
    )(key, rank_of_cell, out_key, weight, noise)


def solution(mesh):
    in_specs = (P("blk", None, None), P("blk", None), P("blk"), P("col", "blk"))
    out_specs = P("col", "blk")
    return jax.shard_map(local, mesh=mesh, in_specs=in_specs, out_specs=out_specs, check_vma=False)
```

time: 842 us -> 156 us (0.19)
  blocking collectives: 414 us -> 0 us
  other arithmetic: 271 us -> 1.04 us
  Pallas kernels: 0 us -> 152 us
  waiting for transfers between devices: 44.5 us -> 0 us
  loops' own time: 36.3 us -> 0 us
  matrix products: 31.3 us -> 0 us
  local copies, waits for them, and re-layouts: 28.4 us -> 2.76 us
  between operations: 14 us -> 0.07 us
    all_gather x9 -> x0, blocking collectives: 414 us -> none  [the longest x7 345 us: local(): gathered = lax.all_gather(packed, 'blk', axis=1, tiled=True)]
    another operation x40 -> x1, other arithmetic: 261 us -> 0.07 us  [local(): mine = jnp.stack([col, col + cols])]
    pallas_call x0 -> x3, Pallas kernels: none -> 152 us  [the longest x1 92.5 us: local(): pl.pallas_call(section_kernel, out_shape=shape(normals.shape, F32), in_sp...]
    all_gather x2 -> x0, waiting for transfers between devices: 43.7 us -> none  [the longest x1 24.4 us: local(): part_coords = lax.all_gather(coords, 'blk', axis=0, tiled=True)]
    another operation x3 -> x0, loops' own time: 36.3 us -> none  [the longest x1 36.1 us: assemble_every_factor(): lax.map(lambda triple: factor(triple[0], triple[1], triple[2]), inputs)]
    dot_general x12 -> x0, matrix products: 19.7 us -> none  [the longest x8 17 us: local(): jnp.einsum('rga,jra->jrg', weights, near_vals.reshape(columns, resident_b...]
    another operation x34 -> x0, local copies, waits for them, and re-layouts: 15.5 us -> none
    another operation x40 -> x0, matrix products: 11.6 us -> none  [the longest x14 3.97 us: factor(): lax.linalg.triangular_solve(chol_near, whitened, left_side=True, lower=Tr...]
  transfers between devices with their start and end apart: 2 -> 0, of which waited for: 2 -> 0; matrix products, arithmetic and copies ran while one was open for 1% -> 0% of each run, Pallas kernels for 0% -> 0%
where the time goes in v1:
time: 156 us
  Pallas kernels  152 us (97%)
  local copies, waits for them, and re-layouts  2.76 us (2%)
    pallas_call x1, Pallas kernels, local(): pl.pallas_call(section_kernel, out_shape=shape(normals.shape, F32), in_sp...  92.5 us
    pallas_call x1, Pallas kernels, local(): pl.pallas_call(factor_kernel, out_shape=(shape((2, K * B, B), F32), shape...  34.2 us
    pallas_call x1, Pallas kernels, local(): pl.pallas_call(exchange_kernel, out_shape=(shape((2, 8, B), F32), shape((...  25 us

profile of v1, /device:TPU:1, one launch (start us, length us, event | category | flops | bytes accessed | tf_op | source)
XLA Modules:
  0.0 155.6 jit_solution(11640561175706778729)
XLA Ops:
  0.0 0.0 copy-start.2
  0.0 0.1 pad_add_fusion
  0.1 0.6 copy-done.2
  0.7 0.2 convert_reduce_fusion
  0.8 0.2 fusion.2.slot_ref
  1.0 0.1 compare_convert_fusion
  1.1 0.1 select_reduce_fusion.1.slot_ref
  1.2 0.0 copy-start.3
  1.2 0.1 select_reduce_fusion.rank_ref
  1.3 0.6 copy-done.3
  1.9 0.1 multiply_reduce_fusion.1
  2.1 0.1 sub.12
  2.2 0.1 broadcast_in_dim.7.ids_ref
  2.2 0.1 broadcast_in_dim.6.code_ref
  2.3 0.1 fusion
  2.4 0.1 multiply_reduce_fusion
  2.5 0.1 copy.9
  2.6 0.1 sub.14
  2.7 0.5 copy-done.1
  3.2 0.1 copy-done
  3.3 25.0 %exchange.1 = (f32[2,8,128]{2,1,0:T(8,128)S(1)}, s32[8,128]{1,0:T(8,128)S(1)}, f32[4,8,128]{2,1,0:T(8,128)S(1)}) custom-call(s32[8]{0:T(128)S(1)} %select_reduce_fusion.1.slot_ref, f32[8,2,128]{2,1,0:T(2,128)S(1)} %copy-done, f32[8,128]{1,0:T(8,128)S(1)} %broadcast_in_dim.6.code_ref, s32[8,128]{1,0:T(8,128)S(1)} %broadcast_in_dim.7.ids_ref, ...), custom_call_target="tpu_custom_call" | custom-call | tf_op jit(solution)/shard_map/exchange/pallas_call | solution.py:563
  28.3 34.2 %factor.1 = (f32[2,512,128]{2,1,0:T(8,128)S(1)}, f32[4,8,128]{2,1,0:T(8,128)S(1)}) custom-call(s32[2]{0:T(128)S(1)} %fusion.2.slot_ref, s32[8]{0:T(128)S(1)} %compare_convert_fusion.1.there_ref, f32[8,2,128]{2,1,0:T(2,128)S(1)} %copy-done, f32[2,8,128]{2,1,0:T(8,128)S(1)} %get-tuple-element.11.near_ref, f32[4,8,128]{2,1,0:T(8,128)S(1)} %get-tuple-element.12.draws_ref), custom_call_target="tpu_custom_call" | custom-call | tf_op jit(solution)/shard_map/factor/pallas_call | solution.py:586
  62.5 92.5 %sections.1 = f32[4,1024]{1,0:T(4,128)S(1)} custom-call(s32[8,128]{1,0:T(8,128)S(1)} %get-tuple-element.10.key_ref, s32[16]{0:T(128)S(1)} %select_reduce_fusion.rank_ref, s32[8]{0:T(128)S(1)} %get-tuple-element.17.out_key_ref, f32[2,512,128]{2,1,0:T(8,128)S(1)} %get-tuple-element.13.weight_ref, f32[4,8,128]{2,1,0:T(8,128)S(1)} %get-tuple-element.14.noise_ref), custom_call_target="tpu_custom_call" | custom-call | tf_op jit(solution)/shard_map/sections/pallas_call | solution.py:596
  155.0 0.6 copy.11
  (9 shorter events, 0.0 us)
Async XLA Ops:
  0.0 0.7 copy-start.2
  1.2 0.7 copy-start.3
  2.5 0.7 copy-start.1
  2.5 0.7 copy-start

commit v2 on v1

v2 whole, which is shorter than its diff:
```python
import jax
import jax.numpy as jnp
from jax import lax
from jax.experimental import pallas as pl
from jax.experimental.pallas import tpu as pltpu
from jax.sharding import PartitionSpec as P

K = 4
SECTIONS = 8
CAP = 2
B = 128
ROUNDS = SECTIONS - 1
LINE = 8
ZERO_TILE = ROUNDS * 2 * LINE * CAP

length_scale = 0.5
nugget_var = 0.1

HIGHEST = lax.Precision.HIGHEST
F32 = jnp.float32
BF16 = jnp.bfloat16


def iota(shape, dim):
    return lax.broadcasted_iota(jnp.int32, shape, dim)


def place():
    blk = lax.axis_index("blk")
    core = blk % 2
    y = (blk // 2) % LINE
    z = blk // (2 * LINE)
    along = (1 - core) * z + core * y
    across = (1 - core) * y + core * z
    return core, along, across


def device_at(core, along, across, other_core):
    chip = (1 - core) * (along * LINE + across) + core * (across * LINE + along)
    return chip * 2 + other_core


FAR_FIRST = (4, 3, 5, 2, 6, 1, 7)


def line_targets(core, along, across):
    targets = []
    for d in FAR_FIRST + (0,):
        if d:
            targets.append((device_at(core, (along + d) % LINE, across, core), 2 * along + core))
        targets.append((device_at(core, along, (across + d) % LINE, 1 - core), 2 * across + core))
    return targets


def line_sources(core, along, across):
    same = [device_at(core, (along + d) % LINE, across, core) for d in range(1, LINE)]
    other = [device_at(core, (along + d) % LINE, across, 1 - core) for d in range(LINE)]
    return same + other


def cross_peers(core, along, across):
    return [
        (device_at(core, along, (across + d) % LINE, core), (across + d) % LINE) for d in FAR_FIRST
    ]


def greet(core, along, across):
    barrier = pltpu.get_barrier_semaphore()
    col = lax.axis_index("col")
    cols = lax.axis_size("col")
    mesh_id = pl.DeviceIdType.MESH
    sources = line_sources(core, along, across) + [device for device, _ in cross_peers(core, along, across)]
    for device in sources:
        pl.semaphore_signal(barrier, inc=1, device_id={"blk": device}, device_id_type=mesh_id)
    for d in range(1, cols):
        pl.semaphore_signal(barrier, inc=1, device_id={"col": (col + d) % cols}, device_id_type=mesh_id)
    return len(sources) + cols - 1


def await_answers(count):
    pl.semaphore_wait(pltpu.get_barrier_semaphore(), count)


def remote(src, dst, send_sem, recv_sem, device_id):
    return pltpu.make_async_remote_copy(
        src_ref=src,
        dst_ref=dst,
        send_sem=send_sem,
        recv_sem=recv_sem,
        device_id=device_id,
        device_id_type=pl.DeviceIdType.MESH,
    )


def wait_bytes(ref, sem):
    pltpu.make_async_copy(ref, ref, sem).wait()


def exchange_kernel(
    slot_ref,
    coords_ref,
    code_ref,
    ids_ref,
    asked_ref,
    normals_ref,
    near_ref,
    key_ref,
    draws_ref,
    own_a,
    own_b,
    own_n,
    got_a,
    got_b,
    got_n,
    picked,
    got_p,
    send_sems,
    recv_sems,
):
    core, along, across = place()
    answers = greet(core, along, across)
    col = lax.axis_index("col")
    cols = lax.axis_size("col")
    my_slot = 2 * along + core
    own_a[0] = coords_ref[:, 0, :]
    own_a[1] = coords_ref[:, 1, :]
    own_a[2] = code_ref[...]
    own_b[0] = ids_ref[...]
    own_b[1] = asked_ref[...]
    for owner in range(cols):
        for half in range(2):
            slot = slot_ref[owner + half * cols]
            drawn = jnp.zeros((4, B), F32)
            for at in range(LINE):
                drawn = drawn + normals_ref[:, at * B : (at + 1) * B] * (slot == at).astype(F32)
            own_n[owner, half * 4 : half * 4 + 4, :] = drawn
    await_answers(answers)
    for device, slot in line_targets(core, along, across):
        remote(own_a, got_a.at[slot], send_sems.at[0], recv_sems.at[0], {"blk": device}).start()
    for device, _ in cross_peers(core, along, across):
        remote(own_b, got_b.at[across], send_sems.at[1], recv_sems.at[1], {"blk": device}).start()
    for d in range(1, cols):
        to = (col + d) % cols
        remote(own_n.at[to], got_n.at[col], send_sems.at[2], recv_sems.at[2], {"col": to}).start()
    got_a[my_slot] = own_a[...]
    got_b[across] = own_b[...]
    got_n[col] = own_n[col]
    lane = iota((1, B), 1)
    lane_dev = device_at(core, lane // (2 * LINE), across, (lane // LINE) % 2)
    lane_block = lane_dev * LINE + lane % LINE
    sub = iota((LINE, B), 0)
    entry_half = (iota((1, B), 1) // K) % 2
    wait_bytes(got_a.at[pl.ds(0, 2 * LINE - 1)], recv_sems.at[0])
    wait_bytes(got_b.at[pl.ds(0, LINE - 1)], recv_sems.at[1])
    chosen = jnp.concatenate(
        [(got_b[peer, 0] == lane_block).astype(F32) for peer in range(LINE)], axis=0
    )
    for axis in range(2):
        held = got_a[:, axis].reshape(B, B)
        moved = jnp.dot(chosen, held, precision=HIGHEST, preferred_element_type=F32)
        picked[:, axis] = moved.reshape(LINE, LINE, B)
    for device, peer in cross_peers(core, along, across):
        remote(picked.at[peer], got_p.at[across], send_sems.at[3], recv_sems.at[3], {"blk": device}).start()
    got_p[across] = picked[across]
    sums = [jnp.zeros((LINE, B), jnp.int32) for _ in range(LINE)]
    for dev in range(2 * LINE):
        block = device_at(core, dev // 2, across, dev % 2) * LINE + sub
        value = got_a[dev, 2].astype(jnp.int32) + (2 * dev + 1)
        for peer in range(LINE):
            sums[peer] = sums[peer] + jnp.where(block == got_b[peer, 1], value, 0)
    for peer in range(LINE):
        total = jnp.sum(sums[peer], axis=0, keepdims=True)
        value = total - 1
        turned = value + entry_half * (1 - 2 * (value % 2))
        key_ref[peer : peer + 1, :] = jnp.where(total > 0, turned, ZERO_TILE)
    wait_bytes(got_n.at[pl.ds(0, cols - 1)], recv_sems.at[2])
    draws_ref[...] = got_n[...]
    wait_bytes(got_p.at[pl.ds(0, LINE - 1)], recv_sems.at[3])
    for axis in range(2):
        near = got_p[0, axis]
        for peer in range(1, LINE):
            near = near + got_p[peer, axis]
        near_ref[axis] = near
    wait_bytes(got_a.at[pl.ds(0, 2 * LINE - 1)], send_sems.at[0])
    wait_bytes(got_b.at[pl.ds(0, LINE - 1)], send_sems.at[1])
    wait_bytes(got_n.at[pl.ds(0, cols - 1)], send_sems.at[2])
    wait_bytes(got_p.at[pl.ds(0, LINE - 1)], send_sems.at[3])


def split3(x):
    high = x.astype(BF16).astype(F32)
    rest = x - high
    middle = rest.astype(BF16).astype(F32)
    return high, middle, rest - middle


def thin_product(left, right):
    l1, l2, l3 = split3(left)
    r1, r2, r3 = split3(right)
    tall_left = jnp.concatenate([l1, l1, l2, l2, l1, l3], axis=0).astype(BF16)
    tall_right = jnp.concatenate([r1, r2, r1, r2, r3, r1], axis=0).astype(BF16)
    return lax.dot_general(tall_left, tall_right, (((0,), (0,)), ((), ())), preferred_element_type=F32)


def spread(tile, first):
    return [jnp.broadcast_to(tile[:, first + j : first + j + 1], (8, B)) for j in range(8)]


def weighted_rows(factors, rows):
    terms = [factors[j] * rows[j : j + 1, :] for j in range(8)]
    return ((terms[0] + terms[1]) + (terms[2] + terms[3])) + ((terms[4] + terms[5]) + (terms[6] + terms[7]))


def eliminate(rows, columns, sub):
    columns = list(columns)
    full = rows
    scales = []
    for j in range(8):
        below, here = sub > j, sub == j
        pivot = columns[j][j : j + 1, :]
        inverse = 1.0 / pivot
        factors = columns[j] * inverse
        under = jnp.where(below, factors, 0.0)
        scaled = full[j : j + 1, :] * inverse
        full = jnp.where(here, scaled, full - columns[j] * scaled)
        rows = rows - under * rows[j : j + 1, :]
        for later in range(j + 1, 8):
            columns[later] = jnp.where(
                here, columns[later] * inverse, columns[later] - factors * columns[later][j : j + 1, :]
            )
        scales.append(lax.rsqrt(pivot))
    scale = scales[7]
    for j in range(7):
        scale = jnp.where(sub == j, scales[j], scale)
    return rows * scale, full


def panel_factors(matrices, inverted):
    sub, lane = iota((8, B), 0), iota((8, B), 1)
    wide = iota((B, B), 1)
    matrices = list(matrices)
    ahead = [m[0:8] for m in matrices]
    panels = [[] for _ in matrices]
    for panel in range(B // 8):
        at = 8 * panel
        inside = (lane >= at) & (lane < at + 8)
        for q in range(len(matrices)):
            rows, left = ahead[q], matrices[q]
            if inverted[q]:
                unit = jnp.where(lane == sub + at, 1.0, 0.0)
                done, full = eliminate(jnp.where(inside, unit, rows), spread(rows, at), sub)
                panels[q].append(jnp.where(lane < at + 8, done, 0.0))
            else:
                done, full = eliminate(rows, spread(rows, at), sub)
                panels[q].append(jnp.where(lane >= sub + at, done, 0.0))
            if at + 8 < B:
                following = left[at + 8 : at + 16]
                drop = weighted_rows(spread(following, at), full)
                if inverted[q]:
                    following = jnp.where(inside, 0.0, following)
                    left = jnp.where((wide >= at) & (wide < at + 8), 0.0, left)
                ahead[q] = following - drop
                matrices[q] = left - thin_product(done, done)
    return [jnp.concatenate(p, axis=0) for p in panels]


def multiply(left, right):
    return jnp.dot(left, right, precision=HIGHEST, preferred_element_type=F32)


def multiply_tn(left, right):
    return lax.dot_general(
        left, right, (((0,), (0,)), ((), ())), precision=HIGHEST, preferred_element_type=F32
    )


def covariance(row_x, row_y, col_x, col_y):
    dx = col_x - row_x
    dy = col_y - row_y
    return jnp.exp(-jnp.sqrt(dx * dx + dy * dy) / length_scale)


def build_covariances(slot_ref, there_ref, coords_ref, near_ref, cov):
    eye = (iota((B, B), 0) == iota((B, B), 1)).astype(F32)
    for q in range(2):
        own = coords_ref[slot_ref[q]]
        points = [
            (near_ref[0, q * K + k : q * K + k + 1, :], near_ref[1, q * K + k : q * K + k + 1, :])
            for k in range(K)
        ] + [(own[0:1], own[1:2])]
        there = [there_ref[q * K + k].astype(F32) for k in range(K)] + [jnp.float32(1.0)]
        for a in range(K + 1):
            col_x = jnp.broadcast_to(points[a][0], (B, B)).T
            col_y = jnp.broadcast_to(points[a][1], (B, B)).T
            for b in range(a, K + 1):
                block = covariance(points[b][0], points[b][1], col_x, col_y) * (there[a] * there[b])
                if a == b:
                    block = block + (nugget_var * there[a] + (1.0 - there[a])) * eye
                cov[q, a, :, b * B : (b + 1) * B] = block


def sample_kernel(
    key_ref,
    rank_ref,
    out_key_ref,
    slot_ref,
    there_ref,
    coords_ref,
    near_ref,
    draws_ref,
    out_ref,
    cov,
    inverses,
    weights,
    first_noise,
    noise,
    near_first,
    early,
    late,
    got_first,
    got_noise,
    got_near,
    values,
    turned,
    got_line,
    held,
    picked,
    got_cross,
    high,
    low,
    local_sem,
    col_send,
    col_recv,
    line_send,
    line_recv,
    cross_send,
    cross_recv,
):
    core, along, across = place()
    answers = greet(core, along, across)
    col = lax.axis_index("col")
    cols = lax.axis_size("col")
    peers = [(col + d) % cols for d in range(1, cols)]
    my_slot = 2 * along + core
    sub = iota((8, B), 0)
    rows = draws_ref.shape[0] * draws_ref.shape[1]
    draws = draws_ref[...].reshape(rows, B)
    held[ZERO_TILE] = jnp.zeros((8, B), F32)

    def to_peers(source, target, which):
        for to in peers:
            remote(source(to), target.at[col], col_send.at[which], col_recv.at[which], {"col": to}).start()

    def from_peers(target, sems, which):
        wait_bytes(target.at[pl.ds(0, cols - 1)], sems.at[which])

    def noise_of(section, tiles_ref):
        tiles = []
        for slot in range(CAP):
            rank = jnp.maximum(rank_ref[CAP * section + slot], 0)
            tile = tiles_ref[rank % cols]
            swapped = pltpu.roll(tile, 4, 0)
            keep = (rank // cols == slot).astype(F32)
            tiles.append(tile * keep + swapped * (1.0 - keep))
        return jnp.where(sub < 4, tiles[0], tiles[1])

    def spread_values(s, tile):
        values[s] = tile
        turned[CAP * s] = tile
        turned[CAP * s + 1] = pltpu.roll(tile, 4, 0)

    def prepare(section, both):
        for slot in range(CAP):
            rank = jnp.maximum(rank_ref[CAP * section + slot], 0)
            place_in_wave = rank % cols
            weight = early[place_in_wave]
            if both:
                is_late = (rank // cols).astype(F32)
                weight = weight * (1.0 - is_late) + late[place_in_wave] * is_late
            part = weight.astype(BF16)
            high[:, slot * B : (slot + 1) * B] = part
            low[:, slot * B : (slot + 1) * B] = (weight - part.astype(F32)).astype(BF16)

    def share(s):
        for device, slot in line_targets(core, along, across):
            remote(
                values.at[s], got_line.at[s, slot], line_send.at[s], line_recv.at[s], {"blk": device}
            ).start()
        got_line[s, my_slot] = values[s]

    def pass_on(s):
        wait_bytes(got_line.at[s, pl.ds(0, 2 * LINE - 1)], line_recv.at[s])
        first = s * (2 * LINE * CAP)
        for dev in range(2 * LINE):
            tile = got_line[s, dev]
            held[first + 2 * dev] = tile
            held[first + 2 * dev + 1] = pltpu.roll(tile, 4, 0)

        def pick(peer, slot_there):
            lanes = (s + 1) * (CAP * K)
            for k in range(K):
                upper = held[key_ref[peer, lanes + k]]
                lower = held[key_ref[peer, lanes + K + k]]
                slot_there[k] = jnp.where(sub < 4, upper, lower)

        for device, peer in cross_peers(core, along, across):
            pick(peer, picked.at[s, peer])
            remote(
                picked.at[s, peer], got_cross.at[s, across], cross_send.at[s], cross_recv.at[s], {"blk": device}
            ).start()
        pick(across, got_cross.at[s, across])

    def collect(s):
        wait_bytes(got_cross.at[s, pl.ds(0, LINE - 1)], cross_recv.at[s])
        near = []
        for k in range(K):
            tiles = [got_cross[s, peer, k] for peer in range(LINE)]
            while len(tiles) > 1:
                tiles = [tiles[i] + tiles[i + 1] for i in range(0, len(tiles), 2)]
            near.append(tiles[0])
        return jnp.concatenate(near, axis=1)

    def update(s, near):
        part = near.astype(BF16).astype(F32)
        both = jnp.concatenate([part, near - part], axis=0).astype(BF16)
        first = jnp.dot(both, high[...], preferred_element_type=F32)
        second = jnp.dot(both[0:8], low[...], preferred_element_type=F32)
        total = first[0:8] + (first[8:16] + second)
        added = jnp.where(sub < 4, total[:, :B], total[:, B:])
        spread_values(s, added + noise_of(s, got_noise))

    build_covariances(slot_ref, there_ref, coords_ref, near_ref, cov)
    own_cov = cov[0, K, :, K * B :]
    first_noise[...] = multiply(draws, panel_factors([own_cov], [False])[0]).reshape(first_noise.shape)
    await_answers(answers)
    to_peers(lambda to: first_noise.at[to], got_first, 0)
    got_first[col] = first_noise[col]

    def after_first():
        from_peers(got_first, col_recv, 0)
        spread_values(0, noise_of(0, got_first))
        share(0)

    def after_second():
        pass_on(0)

    def after_third():
        near_first[...] = collect(0)
        to_peers(lambda to: near_first, got_near, 1)
        got_near[col] = near_first[...]

    def after_fourth():
        pass

    between = (after_first, after_second, after_third, after_fourth)

    def step(k, carry):
        start = pl.multiple_of(k * B, B)
        inverse = panel_factors([cov[q, k, :, pl.ds(start, B)] for q in range(2)], [True, True])
        for q in range(2):
            inverses[q, k] = inverse[q]
        for at in range(K):

            @pl.when(k == at)
            def _(at=at):
                for q in range(2):
                    rest = slice((at + 1) * B, (K + 1) * B)
                    white = multiply(inverse[q], cov[q, at, :, rest])
                    cov[q, at, :, rest] = white
                    for row in range(at + 1, K + 1):
                        first = (row - at - 1) * B
                        cov[q, row, :, row * B :] = cov[q, row, :, row * B :] - multiply_tn(
                            white[:, first : first + B], white[:, first:]
                        )
                between[at]()

        return carry

    lax.fori_loop(0, K, step, 0)
    upper = panel_factors([cov[q, K, :, K * B :] for q in range(2)], [False, False])
    for q in range(2):
        for k in reversed(range(K)):
            total = cov[q, k, :, K * B :]
            if k + 1 < K:
                total = total - multiply(cov[q, k, :, (k + 1) * B : K * B], weights[q, (k + 1) * B :, :])
            weights[q, k * B : (k + 1) * B, :] = multiply_tn(inverses[q, k], total)
    drawn = multiply(draws, jnp.concatenate(upper, axis=1))
    from_peers(got_near, col_recv, 1)
    upper_rows = (iota((rows, K * B), 0) // 4) % 2 == 0
    near = got_near[...].reshape(rows, K * B)
    near_slots = [near, pltpu.roll(near, rows - 4, 0)]
    chosen = jnp.zeros((rows, K * B), F32)
    for slot in range(CAP):
        chosen = chosen + near_slots[slot] * (rank_ref[CAP + slot] == col).astype(F32)
    known = multiply(jnp.where(upper_rows, chosen, 0.0), weights[0])
    mine = jnp.where(upper_rows[:, :B], drawn[:, :B], drawn[:, B:]) + known
    noise[...] = mine.reshape(noise.shape)
    to_peers(lambda to: noise.at[to], got_noise, 2)
    got_noise[col] = noise[col]
    for wave, buffer in ((0, early), (1, late)):
        to_peers(lambda to, wave=wave: weights.at[wave], buffer, 3 + wave)
        pltpu.make_async_copy(weights.at[wave], buffer.at[col], local_sem.at[wave]).start()
    from_peers(got_noise, col_recv, 2)
    spread_values(1, noise_of(1, got_noise))
    share(1)
    pass_on(1)
    from_peers(early, col_recv, 3)
    pltpu.make_async_copy(weights.at[0], early.at[col], local_sem.at[0]).wait()
    from_peers(late, col_recv, 4)
    pltpu.make_async_copy(weights.at[1], late.at[col], local_sem.at[1]).wait()
    prepare(2, True)
    update(2, collect(1))
    share(2)

    def section(s, carry):
        prepare(s + 1, True)
        pass_on(s)
        update(s + 1, collect(s))

        @pl.when(s + 1 < ROUNDS)
        def _():
            share(s + 1)

        return carry

    lax.fori_loop(2, ROUNDS, section, 0)
    for block in range(out_ref.shape[1] // B):
        out_ref[:, block * B : (block + 1) * B] = turned[out_key_ref[block]][0:4]
    from_peers(got_first, col_send, 0)
    from_peers(got_near, col_send, 1)
    from_peers(got_noise, col_send, 2)
    from_peers(early, col_send, 3)
    from_peers(late, col_send, 4)

    def finish(s, carry):
        wait_bytes(got_line.at[s, pl.ds(0, 2 * LINE - 1)], line_send.at[s])
        wait_bytes(got_cross.at[s, pl.ds(0, LINE - 1)], cross_send.at[s])
        return carry

    lax.fori_loop(0, ROUNDS, finish, 0)


VMEM_SPEC = pl.BlockSpec(memory_space=pltpu.VMEM)
SMEM_SPEC = pl.BlockSpec(memory_space=pltpu.SMEM)
VMEM_LIMIT = 40 * 1024 * 1024


def local(coords, neighbours, sections, normals):
    blocks = coords.shape[0]
    cols = lax.axis_size("col")
    col = lax.axis_index("col")
    i32 = jnp.int32
    slots = jnp.arange(blocks, dtype=i32)
    same = sections[None, :] == sections[:, None]
    lower = sections[None, :] < sections[:, None]
    earlier = slots[None, :] < slots[:, None]
    within = jnp.sum((same & earlier).astype(i32), axis=1)
    rank = jnp.sum((lower | (same & earlier)).astype(i32), axis=1)
    by_rank = rank[None, :] == slots[:, None]
    slot_of_rank = jnp.sum(by_rank.astype(i32) * slots[None, :], axis=1)
    cells = jnp.arange(SECTIONS * CAP, dtype=i32)
    in_cell = cells[:, None] == (sections * CAP + within)[None, :]
    rank_of_cell = jnp.sum(in_cell.astype(i32) * (rank + 1)[None, :], axis=1) - 1
    listed = neighbours + 1
    asked = jnp.sum(in_cell.astype(i32)[:, :, None] * listed[None, :, :], axis=1).reshape(-1) - 1
    asked = jnp.pad(asked, (0, B - asked.shape[0]), constant_values=-1)
    mine = jnp.stack([col, col + cols])
    is_mine = rank[None, :] == mine[:, None]
    my_slots = jnp.sum(is_mine.astype(i32) * slots[None, :], axis=1)
    ids = jnp.sum(is_mine.astype(i32)[:, :, None] * listed[None, :, :], axis=1).reshape(-1) - 1
    there = (ids >= 0).astype(i32)
    code = (sections * (2 * LINE * CAP) + within).astype(F32)
    out_key = sections * CAP + within

    def tile(v):
        return jnp.broadcast_to(v[:, None], (blocks, B))

    shape = jax.ShapeDtypeStruct
    near, key, draws = pl.pallas_call(
        exchange_kernel,
        out_shape=(shape((2, 8, B), F32), shape((LINE, B), i32), shape((cols, 8, B), F32)),
        in_specs=[SMEM_SPEC] + [VMEM_SPEC] * 5,
        out_specs=(VMEM_SPEC,) * 3,
        scratch_shapes=[
            pltpu.VMEM((3, 8, B), F32),
            pltpu.VMEM((2, 8, B), i32),
            pltpu.VMEM((cols, 8, B), F32),
            pltpu.VMEM((2 * LINE, 3, 8, B), F32),
            pltpu.VMEM((LINE, 2, 8, B), i32),
            pltpu.VMEM((cols, 8, B), F32),
            pltpu.VMEM((LINE, 2, 8, B), F32),
            pltpu.VMEM((LINE, 2, 8, B), F32),
            pltpu.SemaphoreType.DMA((4,)),
            pltpu.SemaphoreType.DMA((4,)),
        ],
        compiler_params=pltpu.CompilerParams(
            collective_id=0, has_side_effects=True, vmem_limit_bytes=VMEM_LIMIT
        ),
        name="exchange",
    )(slot_of_rank, coords, tile(code), tile(ids), jnp.broadcast_to(asked[None, :], (8, B)), normals)

    return pl.pallas_call(
        sample_kernel,
        out_shape=shape(normals.shape, F32),
        in_specs=[SMEM_SPEC] * 5 + [VMEM_SPEC] * 3,
        out_specs=VMEM_SPEC,
        scratch_shapes=[
            pltpu.VMEM((2, K + 1, B, (K + 1) * B), F32),
            pltpu.VMEM((2, K, B, B), F32),
            pltpu.VMEM((2, K * B, B), F32),
            pltpu.VMEM((cols, 8, B), F32),
            pltpu.VMEM((cols, 8, B), F32),
            pltpu.VMEM((8, K * B), F32),
            pltpu.VMEM((cols, K * B, B), F32),
            pltpu.VMEM((cols, K * B, B), F32),
            pltpu.VMEM((cols, 8, B), F32),
            pltpu.VMEM((cols, 8, B), F32),
            pltpu.VMEM((cols, 8, K * B), F32),
            pltpu.VMEM((SECTIONS, 8, B), F32),
            pltpu.VMEM((SECTIONS * CAP, 8, B), F32),
            pltpu.VMEM((ROUNDS, 2 * LINE, 8, B), F32),
            pltpu.VMEM((ZERO_TILE + 1, 8, B), F32),
            pltpu.VMEM((ROUNDS, LINE, K, 8, B), F32),
            pltpu.VMEM((ROUNDS, LINE, K, 8, B), F32),
            pltpu.VMEM((K * B, CAP * B), BF16),
            pltpu.VMEM((K * B, CAP * B), BF16),
            pltpu.SemaphoreType.DMA((2,)),
            pltpu.SemaphoreType.DMA((5,)),
            pltpu.SemaphoreType.DMA((5,)),
            pltpu.SemaphoreType.DMA((ROUNDS,)),
            pltpu.SemaphoreType.DMA((ROUNDS,)),
            pltpu.SemaphoreType.DMA((ROUNDS,)),
            pltpu.SemaphoreType.DMA((ROUNDS,)),
        ],
        compiler_params=pltpu.CompilerParams(
            collective_id=1, has_side_effects=True, vmem_limit_bytes=VMEM_LIMIT
        ),
        name="sample",
    )(key, rank_of_cell, out_key, my_slots, there, coords, near, draws)


def solution(mesh):
    in_specs = (P("blk", None, None), P("blk", None), P("blk"), P("col", "blk"))
    out_specs = P("col", "blk")
    return jax.shard_map(local, mesh=mesh, in_specs=in_specs, out_specs=out_specs, check_vma=False)
```

time: 156 us -> 141 us (0.904)
  Pallas kernels: 152 us -> 137 us
    pallas_call x2 -> x1, Pallas kernels: 127 us -> 113 us  [local(): pl.pallas_call(sample_kernel, out_shape=shape(normals.shape, F32), in_spe...]
where the time goes in v2:
time: 141 us
  Pallas kernels  137 us (97%)
  local copies, waits for them, and re-layouts  2.76 us (2%)
    pallas_call x1, Pallas kernels, local(): pl.pallas_call(sample_kernel, out_shape=shape(normals.shape, F32), in_spe...  113 us
    pallas_call x1, Pallas kernels, local(): pl.pallas_call(exchange_kernel, out_shape=(shape((2, 8, B), F32), shape((...  24.1 us

profile of v2, /device:TPU:1, one launch (start us, length us, event | category | flops | bytes accessed | tf_op | source)
XLA Modules:
  0.0 140.8 jit_solution(12798839428997813054)
XLA Ops:
  0.0 0.0 copy-start.2
  0.0 0.1 pad_add_fusion
  0.1 0.6 copy-done.2
  0.7 0.2 convert_reduce_fusion
  0.8 0.2 fusion.2.slot_ref
  1.0 0.1 compare_convert_fusion
  1.1 0.1 select_reduce_fusion.1.slot_ref
  1.2 0.0 copy-start.3
  1.2 0.1 select_reduce_fusion
  1.3 0.6 copy-done.3
  1.9 0.1 multiply_reduce_fusion.1
  2.1 0.1 sub.15
  2.2 0.1 broadcast_in_dim.7.ids_ref
  2.2 0.1 broadcast_in_dim.6.code_ref
  2.3 0.1 fusion
  2.4 0.1 multiply_reduce_fusion
  2.5 0.0 copy-start.1
  2.5 0.1 copy.9
  2.6 0.1 sub.17
  2.7 0.5 copy-done.1
  3.2 0.1 copy-done
  3.3 24.1 %exchange.1 = (f32[2,8,128]{2,1,0:T(8,128)S(1)}, s32[8,128]{1,0:T(8,128)S(1)}, f32[4,8,128]{2,1,0:T(8,128)S(1)}) custom-call(s32[8]{0:T(128)S(1)} %select_reduce_fusion.1.slot_ref, f32[8,2,128]{2,1,0:T(2,128)S(1)} %copy-done, f32[8,128]{1,0:T(8,128)S(1)} %broadcast_in_dim.6.code_ref, s32[8,128]{1,0:T(8,128)S(1)} %broadcast_in_dim.7.ids_ref, ...), custom_call_target="tpu_custom_call" | custom-call | tf_op jit(solution)/shard_map/exchange/pallas_call | solution.py:579
  27.3 112.8 %sample.1 = f32[4,1024]{1,0:T(4,128)S(1)} custom-call(s32[8,128]{1,0:T(8,128)S(1)} %get-tuple-element.8.key_ref, s32[16]{0:T(128)S(1)} %broadcast_add_fusion.3.rank_ref, s32[8]{0:T(128)S(1)} %get-tuple-element.13.out_key_ref, s32[2]{0:T(128)S(1)} %fusion.2.slot_ref, s32[8]{0:T(128)S(1)} %compare_convert_fusion.1.there_ref, f32[8,2,128]{2,1,0:T(2,128)S(1)} %copy-done, ...), custom_call_target="tpu_custom_call" | custom-call | tf_op jit(solution)/shard_map/sample/pallas_call | solution.py:602
  140.2 0.6 copy.11
  (9 shorter events, 0.0 us)
Async XLA Ops:
  0.0 0.7 copy-start.2
  1.2 0.7 copy-start.3
  2.5 0.7 copy-start.1
  2.6 0.7 copy-start

commit v3 on v2

--- a/solution.py
+++ b/solution.py
@@ -203,7 +203,7 @@
 
 
 def spread(tile, first):
-    return [jnp.broadcast_to(tile[:, first + j : first + j + 1], (8, B)) for j in range(8)]
+    return [jnp.take_along_axis(tile, jnp.full((8, B), first + j, jnp.int32), axis=1) for j in range(8)]
 
 
 def weighted_rows(factors, rows):
@@ -312,6 +312,7 @@
     cov,
     inverses,
     weights,
+    first_cov,
     first_noise,
     noise,
     near_first,
@@ -430,33 +431,33 @@
         spread_values(s, added + noise_of(s, got_noise))
 
     build_covariances(slot_ref, there_ref, coords_ref, near_ref, cov)
-    own_cov = cov[0, K, :, K * B :]
-    first_noise[...] = multiply(draws, panel_factors([own_cov], [False])[0]).reshape(first_noise.shape)
-    await_answers(answers)
-    to_peers(lambda to: first_noise.at[to], got_first, 0)
-    got_first[col] = first_noise[col]
-
-    def after_first():
+    first_cov[...] = cov[0, K, :, K * B :]
+
+    def after_first(first_upper):
+        first_noise[...] = multiply(draws, first_upper).reshape(first_noise.shape)
+        await_answers(answers)
+        to_peers(lambda to: first_noise.at[to], got_first, 0)
+        got_first[col] = first_noise[col]
+
+    def after_second(_):
         from_peers(got_first, col_recv, 0)
         spread_values(0, noise_of(0, got_first))
         share(0)
 
-    def after_second():
+    def after_third(_):
         pass_on(0)
 
-    def after_third():
+    def after_fourth(_):
         near_first[...] = collect(0)
         to_peers(lambda to: near_first, got_near, 1)
         got_near[col] = near_first[...]
 
-    def after_fourth():
-        pass
-
     between = (after_first, after_second, after_third, after_fourth)
 
     def step(k, carry):
         start = pl.multiple_of(k * B, B)
-        inverse = panel_factors([cov[q, k, :, pl.ds(start, B)] for q in range(2)], [True, True])
+        matrices = [cov[q, k, :, pl.ds(start, B)] for q in range(2)] + [first_cov[...]]
+        *inverse, first_upper = panel_factors(matrices, [True, True, False])
         for q in range(2):
             inverses[q, k] = inverse[q]
         for at in range(K):
@@ -472,7 +473,7 @@
                         cov[q, row, :, row * B :] = cov[q, row, :, row * B :] - multiply_tn(
                             white[:, first : first + B], white[:, first:]
                         )
-                between[at]()
+                between[at](first_upper)
 
         return carry
 
@@ -506,11 +507,11 @@
     pass_on(1)
     from_peers(early, col_recv, 3)
     pltpu.make_async_copy(weights.at[0], early.at[col], local_sem.at[0]).wait()
+    prepare(2, False)
+    update(2, collect(1))
+    share(2)
     from_peers(late, col_recv, 4)
     pltpu.make_async_copy(weights.at[1], late.at[col], local_sem.at[1]).wait()
-    prepare(2, True)
-    update(2, collect(1))
-    share(2)
 
     def section(s, carry):
         prepare(s + 1, True)
@@ -608,6 +609,7 @@
             pltpu.VMEM((2, K + 1, B, (K + 1) * B), F32),
             pltpu.VMEM((2, K, B, B), F32),
             pltpu.VMEM((2, K * B, B), F32),
+            pltpu.VMEM((B, B), F32),
             pltpu.VMEM((cols, 8, B), F32),
             pltpu.VMEM((cols, 8, B), F32),
             pltpu.VMEM((8, K * B), F32),

time: 141 us -> 133 us (0.943)
  Pallas kernels: 137 us -> 129 us
    pallas_call x1, Pallas kernels: 113 us -> 105 us  [local(): pl.pallas_call(sample_kernel, out_shape=shape(normals.shape, F32), in_spe...]
where the time goes in v3:
time: 133 us
  Pallas kernels  129 us (97%)
  local copies, waits for them, and re-layouts  2.76 us (2%)
    pallas_call x1, Pallas kernels, local(): pl.pallas_call(sample_kernel, out_shape=shape(normals.shape, F32), in_spe...  105 us
    pallas_call x1, Pallas kernels, local(): pl.pallas_call(exchange_kernel, out_shape=(shape((2, 8, B), F32), shape((...  24.1 us

profile of v3, /device:TPU:1, one launch (start us, length us, event | category | flops | bytes accessed | tf_op | source)
XLA Modules:
  0.0 132.9 jit_solution(16271132236553463684)
XLA Ops:
  0.0 0.0 copy-start.2
  0.0 0.1 pad_add_fusion
  0.1 0.6 copy-done.2
  0.7 0.2 convert_reduce_fusion
  0.8 0.2 fusion.2.slot_ref
  1.0 0.1 compare_convert_fusion
  1.1 0.1 select_reduce_fusion.1.slot_ref
  1.2 0.0 copy-start.3
  1.2 0.1 select_reduce_fusion
  1.3 0.6 copy-done.3
  1.9 0.1 multiply_reduce_fusion.1
  2.1 0.1 sub.15
  2.2 0.1 broadcast_in_dim.7.ids_ref
  2.2 0.1 broadcast_in_dim.6.code_ref
  2.3 0.1 fusion
  2.4 0.1 multiply_reduce_fusion
  2.5 0.0 copy-start.1
  2.5 0.1 copy.9
  2.6 0.1 sub.17
  2.7 0.5 copy-done.1
  3.2 0.1 copy-done
  3.3 24.1 %exchange.1 = (f32[2,8,128]{2,1,0:T(8,128)S(1)}, s32[8,128]{1,0:T(8,128)S(1)}, f32[4,8,128]{2,1,0:T(8,128)S(1)}) custom-call(s32[8]{0:T(128)S(1)} %select_reduce_fusion.1.slot_ref, f32[8,2,128]{2,1,0:T(2,128)S(1)} %copy-done, f32[8,128]{1,0:T(8,128)S(1)} %broadcast_in_dim.6.code_ref, s32[8,128]{1,0:T(8,128)S(1)} %broadcast_in_dim.7.ids_ref, ...), custom_call_target="tpu_custom_call" | custom-call | tf_op jit(solution)/shard_map/exchange/pallas_call | solution.py:580
  27.3 104.9 %sample.1 = f32[4,1024]{1,0:T(4,128)S(1)} custom-call(s32[8,128]{1,0:T(8,128)S(1)} %get-tuple-element.8.key_ref, s32[16]{0:T(128)S(1)} %broadcast_add_fusion.3.rank_ref, s32[8]{0:T(128)S(1)} %get-tuple-element.13.out_key_ref, s32[2]{0:T(128)S(1)} %fusion.2.slot_ref, s32[8]{0:T(128)S(1)} %compare_convert_fusion.1.there_ref, f32[8,2,128]{2,1,0:T(2,128)S(1)} %copy-done, ...), custom_call_target="tpu_custom_call" | custom-call | tf_op jit(solution)/shard_map/sample/pallas_call | solution.py:603
  132.3 0.6 copy.11
  (9 shorter events, 0.0 us)
Async XLA Ops:
  0.0 0.7 copy-start.2
  1.2 0.7 copy-start.3
  2.5 0.7 copy-start.1
  2.6 0.7 copy-start

commit v4 on v3

--- a/solution.py
+++ b/solution.py
@@ -97,15 +97,17 @@
 
 
 def exchange_kernel(
-    slot_ref,
+    sections_ref,
+    neighbours_ref,
     coords_ref,
-    code_ref,
-    ids_ref,
-    asked_ref,
     normals_ref,
     near_ref,
     key_ref,
     draws_ref,
+    rank_ref,
+    out_key_ref,
+    slot_ref,
+    there_ref,
     own_a,
     own_b,
     own_n,
@@ -122,17 +124,45 @@
     col = lax.axis_index("col")
     cols = lax.axis_size("col")
     my_slot = 2 * along + core
+    sub, lane = iota((8, B), 0), iota((8, B), 1)
+    blocks = range(LINE)
+
+    def flag(condition):
+        return condition.astype(jnp.int32)
+
+    section = [sections_ref[i] for i in blocks]
+    listed = [[neighbours_ref[i, k] for k in range(K)] for i in blocks]
+    within = [sum((flag(section[j] == section[i]) for j in range(i)), jnp.int32(0)) for i in blocks]
+    rank = [within[i] + sum(flag(section[j] < section[i]) for j in blocks) for i in blocks]
+    cell = [section[i] * CAP + within[i] for i in blocks]
+    for c in range(SECTIONS * CAP):
+        rank_ref[c] = sum(flag(cell[i] == c) * (rank[i] + 1) for i in blocks) - 1
+    code = jnp.zeros((8, B), F32)
+    asked = jnp.full((8, B), -1, jnp.int32)
+    for i in blocks:
+        out_key_ref[i] = cell[i]
+        code = jnp.where(sub == i, (section[i] * (2 * LINE * CAP) + within[i]).astype(F32), code)
+        for k in range(K):
+            asked = jnp.where(lane == cell[i] * K + k, listed[i][k], asked)
+    ids = jnp.full((8, B), -1, jnp.int32)
+    for half in range(2):
+        mine = [flag(rank[i] == col + half * cols) for i in blocks]
+        slot_ref[half] = sum(mine[i] * i for i in blocks)
+        for k in range(K):
+            entry = sum(mine[i] * (listed[i][k] + 1) for i in blocks) - 1
+            there_ref[half * K + k] = flag(entry >= 0)
+            ids = jnp.where(sub == half * K + k, entry, ids)
     own_a[0] = coords_ref[:, 0, :]
     own_a[1] = coords_ref[:, 1, :]
-    own_a[2] = code_ref[...]
-    own_b[0] = ids_ref[...]
-    own_b[1] = asked_ref[...]
+    own_a[2] = code
+    own_b[0] = ids
+    own_b[1] = asked
     for owner in range(cols):
         for half in range(2):
-            slot = slot_ref[owner + half * cols]
             drawn = jnp.zeros((4, B), F32)
-            for at in range(LINE):
-                drawn = drawn + normals_ref[:, at * B : (at + 1) * B] * (slot == at).astype(F32)
+            for i in blocks:
+                chosen = (rank[i] == owner + half * cols).astype(F32)
+                drawn = drawn + normals_ref[:, i * B : (i + 1) * B] * chosen
             own_n[owner, half * 4 : half * 4 + 4, :] = drawn
     await_answers(answers)
     for device, slot in line_targets(core, along, across):
@@ -312,7 +342,6 @@
     cov,
     inverses,
     weights,
-    first_cov,
     first_noise,
     noise,
     near_first,
@@ -320,6 +349,7 @@
     late,
     got_first,
     got_noise,
+    got_later,
     got_near,
     values,
     turned,
@@ -421,102 +451,121 @@
             near.append(tiles[0])
         return jnp.concatenate(near, axis=1)
 
-    def update(s, near):
+    def update(s, near, noise_now):
         part = near.astype(BF16).astype(F32)
         both = jnp.concatenate([part, near - part], axis=0).astype(BF16)
         first = jnp.dot(both, high[...], preferred_element_type=F32)
         second = jnp.dot(both[0:8], low[...], preferred_element_type=F32)
         total = first[0:8] + (first[8:16] + second)
         added = jnp.where(sub < 4, total[:, :B], total[:, B:])
-        spread_values(s, added + noise_of(s, got_noise))
+        spread_values(s, added + noise_now)
 
     build_covariances(slot_ref, there_ref, coords_ref, near_ref, cov)
-    first_cov[...] = cov[0, K, :, K * B :]
-
-    def after_first(first_upper):
-        first_noise[...] = multiply(draws, first_upper).reshape(first_noise.shape)
-        await_answers(answers)
-        to_peers(lambda to: first_noise.at[to], got_first, 0)
-        got_first[col] = first_noise[col]
-
-    def after_second(_):
-        from_peers(got_first, col_recv, 0)
-        spread_values(0, noise_of(0, got_first))
-        share(0)
-
-    def after_third(_):
-        pass_on(0)
-
-    def after_fourth(_):
-        near_first[...] = collect(0)
-        to_peers(lambda to: near_first, got_near, 1)
-        got_near[col] = near_first[...]
-
-    between = (after_first, after_second, after_third, after_fourth)
-
-    def step(k, carry):
-        start = pl.multiple_of(k * B, B)
-        matrices = [cov[q, k, :, pl.ds(start, B)] for q in range(2)] + [first_cov[...]]
-        *inverse, first_upper = panel_factors(matrices, [True, True, False])
-        for q in range(2):
-            inverses[q, k] = inverse[q]
-        for at in range(K):
-
-            @pl.when(k == at)
-            def _(at=at):
-                for q in range(2):
-                    rest = slice((at + 1) * B, (K + 1) * B)
-                    white = multiply(inverse[q], cov[q, at, :, rest])
-                    cov[q, at, :, rest] = white
-                    for row in range(at + 1, K + 1):
-                        first = (row - at - 1) * B
-                        cov[q, row, :, row * B :] = cov[q, row, :, row * B :] - multiply_tn(
-                            white[:, first : first + B], white[:, first:]
-                        )
-                between[at](first_upper)
-
-        return carry
-
-    lax.fori_loop(0, K, step, 0)
-    upper = panel_factors([cov[q, K, :, K * B :] for q in range(2)], [False, False])
-    for q in range(2):
+    def follow(q, k, inverse):
+        rest = slice((k + 1) * B, (K + 1) * B)
+        white = multiply(inverse, cov[q, k, :, rest])
+        cov[q, k, :, rest] = white
+        for row in range(k + 1, K + 1):
+            first = (row - k - 1) * B
+            cov[q, row, :, row * B :] = cov[q, row, :, row * B :] - multiply_tn(
+                white[:, first : first + B], white[:, first:]
+            )
+
+    def back(q):
         for k in reversed(range(K)):
             total = cov[q, k, :, K * B :]
             if k + 1 < K:
                 total = total - multiply(cov[q, k, :, (k + 1) * B : K * B], weights[q, (k + 1) * B :, :])
             weights[q, k * B : (k + 1) * B, :] = multiply_tn(inverses[q, k], total)
-    drawn = multiply(draws, jnp.concatenate(upper, axis=1))
+
+    def send_weights(q, buffer):
+        to_peers(lambda to: weights.at[q], buffer, 4 + q)
+        pltpu.make_async_copy(weights.at[q], buffer.at[col], local_sem.at[q]).start()
+
+    def await_weights(q, buffer):
+        from_peers(buffer, col_recv, 4 + q)
+        pltpu.make_async_copy(weights.at[q], buffer.at[col], local_sem.at[q]).wait()
+
+    def send_noise(q, rows_now):
+        noise[q] = rows_now.reshape(noise.shape[1:])
+        target = (got_noise, got_later)[q]
+        to_peers(lambda to: noise.at[q, to], target, 2 + q)
+        target[col] = noise[q, col]
+
+    inverse, first_upper = panel_factors([cov[0, 0, :, :B], cov[0, K, :, K * B :]], [True, False])
+    inverses[0, 0] = inverse
+    first_noise[...] = multiply(draws, first_upper).reshape(first_noise.shape)
+    await_answers(answers)
+    to_peers(lambda to: first_noise.at[to], got_first, 0)
+    got_first[col] = first_noise[col]
+    follow(0, 0, inverse)
+
+    def step(k, carry):
+        start = pl.multiple_of(k * B, B)
+        behind = pl.multiple_of((k - 1) * B, B)
+        inverse = panel_factors(
+            [cov[0, k, :, pl.ds(start, B)], cov[1, k - 1, :, pl.ds(behind, B)]], [True, True]
+        )
+        inverses[0, k] = inverse[0]
+        inverses[1, k - 1] = inverse[1]
+        for at in range(1, K):
+
+            @pl.when(k == at)
+            def _(at=at):
+                follow(0, at, inverse[0])
+                follow(1, at - 1, inverse[1])
+                if at == 1:
+                    from_peers(got_first, col_recv, 0)
+                    spread_values(0, noise_of(0, got_first))
+                    share(0)
+                elif at == 2:
+                    pass_on(0)
+                else:
+                    near_first[...] = collect(0)
+                    to_peers(lambda to: near_first, got_near, 1)
+                    got_near[col] = near_first[...]
+
+        return carry
+
+    lax.fori_loop(1, K, step, 0)
+    inverse, upper = panel_factors([cov[1, K - 1, :, (K - 1) * B : K * B], cov[0, K, :, K * B :]], [True, False])
+    inverses[1, K - 1] = inverse
+    back(0)
+    drawn = multiply(draws, upper)
     from_peers(got_near, col_recv, 1)
-    upper_rows = (iota((rows, K * B), 0) // 4) % 2 == 0
     near = got_near[...].reshape(rows, K * B)
     near_slots = [near, pltpu.roll(near, rows - 4, 0)]
     chosen = jnp.zeros((rows, K * B), F32)
     for slot in range(CAP):
         chosen = chosen + near_slots[slot] * (rank_ref[CAP + slot] == col).astype(F32)
-    known = multiply(jnp.where(upper_rows, chosen, 0.0), weights[0])
-    mine = jnp.where(upper_rows[:, :B], drawn[:, :B], drawn[:, B:]) + known
-    noise[...] = mine.reshape(noise.shape)
-    to_peers(lambda to: noise.at[to], got_noise, 2)
-    got_noise[col] = noise[col]
-    for wave, buffer in ((0, early), (1, late)):
-        to_peers(lambda to, wave=wave: weights.at[wave], buffer, 3 + wave)
-        pltpu.make_async_copy(weights.at[wave], buffer.at[col], local_sem.at[wave]).start()
+    send_noise(0, drawn + multiply(chosen, weights[0]))
+    send_weights(0, early)
     from_peers(got_noise, col_recv, 2)
     spread_values(1, noise_of(1, got_noise))
     share(1)
+    follow(1, K - 1, inverses[1, K - 1])
+    upper = panel_factors([cov[1, K, :, K * B :]], [False])[0]
     pass_on(1)
-    from_peers(early, col_recv, 3)
-    pltpu.make_async_copy(weights.at[0], early.at[col], local_sem.at[0]).wait()
+    back(1)
+    send_noise(1, multiply(draws, upper))
+    send_weights(1, late)
+    await_weights(0, early)
     prepare(2, False)
-    update(2, collect(1))
+    update(2, collect(1), noise_of(2, got_noise))
     share(2)
-    from_peers(late, col_recv, 4)
-    pltpu.make_async_copy(weights.at[1], late.at[col], local_sem.at[1]).wait()
+    pass_on(2)
+    from_peers(got_later, col_recv, 3)
+    for owner in range(cols):
+        got_first[owner] = jnp.where(sub < 4, got_noise[owner], got_later[owner])
+    await_weights(1, late)
+    prepare(3, True)
+    update(3, collect(2), noise_of(3, got_first))
+    share(3)
 
     def section(s, carry):
         prepare(s + 1, True)
         pass_on(s)
-        update(s + 1, collect(s))
+        update(s + 1, collect(s), noise_of(s + 1, got_first))
 
         @pl.when(s + 1 < ROUNDS)
         def _():
@@ -524,14 +573,15 @@
 
         return carry
 
-    lax.fori_loop(2, ROUNDS, section, 0)
+    lax.fori_loop(3, ROUNDS, section, 0)
     for block in range(out_ref.shape[1] // B):
         out_ref[:, block * B : (block + 1) * B] = turned[out_key_ref[block]][0:4]
     from_peers(got_first, col_send, 0)
     from_peers(got_near, col_send, 1)
     from_peers(got_noise, col_send, 2)
-    from_peers(early, col_send, 3)
-    from_peers(late, col_send, 4)
+    from_peers(got_later, col_send, 3)
+    from_peers(early, col_send, 4)
+    from_peers(late, col_send, 5)
 
     def finish(s, carry):
         wait_bytes(got_line.at[s, pl.ds(0, 2 * LINE - 1)], line_send.at[s])
@@ -547,41 +597,22 @@
 
 
 def local(coords, neighbours, sections, normals):
-    blocks = coords.shape[0]
     cols = lax.axis_size("col")
-    col = lax.axis_index("col")
     i32 = jnp.int32
-    slots = jnp.arange(blocks, dtype=i32)
-    same = sections[None, :] == sections[:, None]
-    lower = sections[None, :] < sections[:, None]
-    earlier = slots[None, :] < slots[:, None]
-    within = jnp.sum((same & earlier).astype(i32), axis=1)
-    rank = jnp.sum((lower | (same & earlier)).astype(i32), axis=1)
-    by_rank = rank[None, :] == slots[:, None]
-    slot_of_rank = jnp.sum(by_rank.astype(i32) * slots[None, :], axis=1)
-    cells = jnp.arange(SECTIONS * CAP, dtype=i32)
-    in_cell = cells[:, None] == (sections * CAP + within)[None, :]
-    rank_of_cell = jnp.sum(in_cell.astype(i32) * (rank + 1)[None, :], axis=1) - 1
-    listed = neighbours + 1
-    asked = jnp.sum(in_cell.astype(i32)[:, :, None] * listed[None, :, :], axis=1).reshape(-1) - 1
-    asked = jnp.pad(asked, (0, B - asked.shape[0]), constant_values=-1)
-    mine = jnp.stack([col, col + cols])
-    is_mine = rank[None, :] == mine[:, None]
-    my_slots = jnp.sum(is_mine.astype(i32) * slots[None, :], axis=1)
-    ids = jnp.sum(is_mine.astype(i32)[:, :, None] * listed[None, :, :], axis=1).reshape(-1) - 1
-    there = (ids >= 0).astype(i32)
-    code = (sections * (2 * LINE * CAP) + within).astype(F32)
-    out_key = sections * CAP + within
-
-    def tile(v):
-        return jnp.broadcast_to(v[:, None], (blocks, B))
-
     shape = jax.ShapeDtypeStruct
-    near, key, draws = pl.pallas_call(
+    near, key, draws, rank_of_cell, out_key, my_slots, there = pl.pallas_call(
         exchange_kernel,
-        out_shape=(shape((2, 8, B), F32), shape((LINE, B), i32), shape((cols, 8, B), F32)),
-        in_specs=[SMEM_SPEC] + [VMEM_SPEC] * 5,
-        out_specs=(VMEM_SPEC,) * 3,
+        out_shape=(
+            shape((2, 8, B), F32),
+            shape((LINE, B), i32),
+            shape((cols, 8, B), F32),
+            shape((SECTIONS * CAP,), i32),
+            shape((LINE,), i32),
+            shape((2,), i32),
+            shape((2 * K,), i32),
+        ),
+        in_specs=[SMEM_SPEC] * 2 + [VMEM_SPEC] * 2,
+        out_specs=(VMEM_SPEC,) * 3 + (SMEM_SPEC,) * 4,
         scratch_shapes=[
             pltpu.VMEM((3, 8, B), F32),
             pltpu.VMEM((2, 8, B), i32),
@@ -598,7 +629,7 @@
             collective_id=0, has_side_effects=True, vmem_limit_bytes=VMEM_LIMIT
         ),
         name="exchange",
-    )(slot_of_rank, coords, tile(code), tile(ids), jnp.broadcast_to(asked[None, :], (8, B)), normals)
+    )(sections, neighbours, coords, normals)
 
     return pl.pallas_call(
         sample_kernel,
@@ -609,12 +640,12 @@
             pltpu.VMEM((2, K + 1, B, (K + 1) * B), F32),
             pltpu.VMEM((2, K, B, B), F32),
             pltpu.VMEM((2, K * B, B), F32),
-            pltpu.VMEM((B, B), F32),
             pltpu.VMEM((cols, 8, B), F32),
-            pltpu.VMEM((cols, 8, B), F32),
+            pltpu.VMEM((2, cols, 8, B), F32),
             pltpu.VMEM((8, K * B), F32),
             pltpu.VMEM((cols, K * B, B), F32),
             pltpu.VMEM((cols, K * B, B), F32),
+            pltpu.VMEM((cols, 8, B), F32),
             pltpu.VMEM((cols, 8, B), F32),
             pltpu.VMEM((cols, 8, B), F32),
             pltpu.VMEM((cols, 8, K * B), F32),
@@ -627,8 +658,8 @@
             pltpu.VMEM((K * B, CAP * B), BF16),
             pltpu.VMEM((K * B, CAP * B), BF16),
             pltpu.SemaphoreType.DMA((2,)),
-            pltpu.SemaphoreType.DMA((5,)),
-            pltpu.SemaphoreType.DMA((5,)),
+            pltpu.SemaphoreType.DMA((6,)),
+            pltpu.SemaphoreType.DMA((6,)),
             pltpu.SemaphoreType.DMA((ROUNDS,)),
             pltpu.SemaphoreType.DMA((ROUNDS,)),
             pltpu.SemaphoreType.DMA((ROUNDS,)),

time: 133 us -> 127 us (0.955)
  Pallas kernels: 129 us -> 123 us
    pallas_call x1, Pallas kernels: 105 us -> 97.9 us  [local(): pl.pallas_call(sample_kernel, out_shape=shape(normals.shape, F32), in_spe...]
    unnamed x9 -> x10, local copies, waits for them, and re-layouts: 2.36 us -> 3.49 us
where the time goes in v4:
time: 127 us; the launch traced here: 126 us
  Pallas kernels  123 us (97%)
  local copies, waits for them, and re-layouts  3.49 us (3%)
    pallas_call x1, Pallas kernels, local(): pl.pallas_call(sample_kernel, out_shape=shape(normals.shape, F32), in_spe...  97.9 us
    pallas_call x1, Pallas kernels, local(): pl.pallas_call(exchange_kernel, out_shape=(shape((2, 8, B), F32), shape((...  24.8 us
    unnamed x10, local copies, waits for them, and re-layouts  3.49 us

profile of v4, /device:TPU:1, one launch (start us, length us, event | category | flops | bytes accessed | tf_op | source)
XLA Modules:
  0.0 126.2 jit_solution(4472248856426474214)
XLA Ops:
  0.0 0.0 copy-start.3
  0.0 0.8 copy.5.neighbours_ref
  0.8 0.0 copy-done.3
  0.8 0.0 copy-start
  0.8 0.7 copy-done
  1.5 0.0 copy-start.2
  1.5 0.7 copy-done.2
  2.2 24.8 %exchange.1 = (f32[2,8,128]{2,1,0:T(8,128)S(1)}, s32[8,128]{1,0:T(8,128)S(1)}, f32[4,8,128]{2,1,0:T(8,128)S(1)}, s32[16]{0:T(128)S(1)}, s32[8]{0:T(128)S(1)}, /*index=5*/s32[2]{0:T(128)S(1)}, s32[8]{0:T(128)S(1)}) custom-call(s32[8]{0:T(128)S(1)} %copy-done.3, s32[8,4]{1,0:T(8,128)S(1)} %copy.5.neighbours_ref, f32[8,2,128]{2,1,0:T(2,128)S(1)} %copy-done, ...), custom_call_target="tpu_custom_call" | custom-call | tf_op jit(solution)/shard_map/exchange/pallas_call | solution.py:603
  27.0 0.0 copy-start.1
  27.0 0.7 copy-done.1
  27.7 97.9 %sample.1 = f32[4,1024]{1,0:T(4,128)S(1)} custom-call(s32[8,128]{1,0:T(8,128)S(1)} %get-tuple-element.12.key_ref, s32[16]{0:T(128)S(1)} %get-tuple-element.13.rank_ref, s32[8]{0:T(128)S(1)} %get-tuple-element.14.out_key_ref, s32[2]{0:T(128)S(1)} %get-tuple-element.15.slot_ref, s32[8]{0:T(128)S(1)} %get-tuple-element.16.there_ref, ...), custom_call_target="tpu_custom_call" | custom-call | tf_op jit(solution)/shard_map/sample/pallas_call | solution.py:634
  125.6 0.6 copy.7
Async XLA Ops:
  0.0 0.8 copy-start.3
  0.8 0.7 copy-start
  1.5 0.7 copy-start.2
  27.0 0.7 copy-start.1

commit v5 on v4

--- a/solution.py
+++ b/solution.py
@@ -99,14 +99,13 @@
 def exchange_kernel(
     sections_ref,
     neighbours_ref,
-    coords_ref,
-    normals_ref,
+    coords_hbm,
+    normals_hbm,
     near_ref,
     key_ref,
     draws_ref,
     rank_ref,
     out_key_ref,
-    slot_ref,
     there_ref,
     own_a,
     own_b,
@@ -116,11 +115,20 @@
     got_n,
     picked,
     got_p,
+    coords_ref,
+    normals_ref,
     send_sems,
     recv_sems,
+    local_sems,
 ):
     core, along, across = place()
     answers = greet(core, along, across)
+    loads = [
+        pltpu.make_async_copy(coords_hbm, coords_ref, local_sems.at[0]),
+        pltpu.make_async_copy(normals_hbm, normals_ref, local_sems.at[1]),
+    ]
+    for load in loads:
+        load.start()
     col = lax.axis_index("col")
     cols = lax.axis_size("col")
     my_slot = 2 * along + core
@@ -145,18 +153,26 @@
         for k in range(K):
             asked = jnp.where(lane == cell[i] * K + k, listed[i][k], asked)
     ids = jnp.full((8, B), -1, jnp.int32)
+    slots = []
     for half in range(2):
         mine = [flag(rank[i] == col + half * cols) for i in blocks]
-        slot_ref[half] = sum(mine[i] * i for i in blocks)
+        slots.append(sum(mine[i] * i for i in blocks))
         for k in range(K):
             entry = sum(mine[i] * (listed[i][k] + 1) for i in blocks) - 1
             there_ref[half * K + k] = flag(entry >= 0)
             ids = jnp.where(sub == half * K + k, entry, ids)
+    loads[0].wait()
     own_a[0] = coords_ref[:, 0, :]
     own_a[1] = coords_ref[:, 1, :]
     own_a[2] = code
+    for axis in range(2):
+        chosen = [
+            jnp.sum(jnp.where(sub == slots[half], own_a[axis], 0.0), axis=0, keepdims=True) for half in range(2)
+        ]
+        near_ref[axis, 8:16, :] = jnp.where(sub == 0, chosen[0], chosen[1])
     own_b[0] = ids
     own_b[1] = asked
+    loads[1].wait()
     for owner in range(cols):
         for half in range(2):
             drawn = jnp.zeros((4, B), F32)
@@ -210,7 +226,7 @@
         near = got_p[0, axis]
         for peer in range(1, LINE):
             near = near + got_p[peer, axis]
-        near_ref[axis] = near
+        near_ref[axis, 0:8, :] = near
     wait_bytes(got_a.at[pl.ds(0, 2 * LINE - 1)], send_sems.at[0])
     wait_bytes(got_b.at[pl.ds(0, LINE - 1)], send_sems.at[1])
     wait_bytes(got_n.at[pl.ds(0, cols - 1)], send_sems.at[2])
@@ -310,14 +326,13 @@
     return jnp.exp(-jnp.sqrt(dx * dx + dy * dy) / length_scale)
 
 
-def build_covariances(slot_ref, there_ref, coords_ref, near_ref, cov):
+def build_covariances(there_ref, near_ref, cov):
     eye = (iota((B, B), 0) == iota((B, B), 1)).astype(F32)
     for q in range(2):
-        own = coords_ref[slot_ref[q]]
         points = [
             (near_ref[0, q * K + k : q * K + k + 1, :], near_ref[1, q * K + k : q * K + k + 1, :])
             for k in range(K)
-        ] + [(own[0:1], own[1:2])]
+        ] + [(near_ref[0, 8 + q : 9 + q, :], near_ref[1, 8 + q : 9 + q, :])]
         there = [there_ref[q * K + k].astype(F32) for k in range(K)] + [jnp.float32(1.0)]
         for a in range(K + 1):
             col_x = jnp.broadcast_to(points[a][0], (B, B)).T
@@ -333,9 +348,7 @@
     key_ref,
     rank_ref,
     out_key_ref,
-    slot_ref,
     there_ref,
-    coords_ref,
     near_ref,
     draws_ref,
     out_ref,
@@ -460,7 +473,7 @@
         added = jnp.where(sub < 4, total[:, :B], total[:, B:])
         spread_values(s, added + noise_now)
 
-    build_covariances(slot_ref, there_ref, coords_ref, near_ref, cov)
+    build_covariances(there_ref, near_ref, cov)
     def follow(q, k, inverse):
         rest = slice((k + 1) * B, (K + 1) * B)
         white = multiply(inverse, cov[q, k, :, rest])
@@ -544,11 +557,11 @@
     spread_values(1, noise_of(1, got_noise))
     share(1)
     follow(1, K - 1, inverses[1, K - 1])
+    back(1)
+    pass_on(1)
+    send_weights(1, late)
     upper = panel_factors([cov[1, K, :, K * B :]], [False])[0]
-    pass_on(1)
-    back(1)
     send_noise(1, multiply(draws, upper))
-    send_weights(1, late)
     await_weights(0, early)
     prepare(2, False)
     update(2, collect(1), noise_of(2, got_noise))
@@ -600,19 +613,18 @@
     cols = lax.axis_size("col")
     i32 = jnp.int32
     shape = jax.ShapeDtypeStruct
-    near, key, draws, rank_of_cell, out_key, my_slots, there = pl.pallas_call(
+    near, key, draws, rank_of_cell, out_key, there = pl.pallas_call(
         exchange_kernel,
         out_shape=(
-            shape((2, 8, B), F32),
+            shape((2, 16, B), F32),
             shape((LINE, B), i32),
             shape((cols, 8, B), F32),
             shape((SECTIONS * CAP,), i32),
             shape((LINE,), i32),
-            shape((2,), i32),
             shape((2 * K,), i32),
         ),
-        in_specs=[SMEM_SPEC] * 2 + [VMEM_SPEC] * 2,
-        out_specs=(VMEM_SPEC,) * 3 + (SMEM_SPEC,) * 4,
+        in_specs=[SMEM_SPEC] * 2 + [pl.BlockSpec(memory_space=pl.ANY)] * 2,
+        out_specs=(VMEM_SPEC,) * 3 + (SMEM_SPEC,) * 3,
         scratch_shapes=[
             pltpu.VMEM((3, 8, B), F32),
             pltpu.VMEM((2, 8, B), i32),
@@ -622,8 +634,11 @@
             pltpu.VMEM((cols, 8, B), F32),
             pltpu.VMEM((LINE, 2, 8, B), F32),
             pltpu.VMEM((LINE, 2, 8, B), F32),
+            pltpu.VMEM(coords.shape, F32),
+            pltpu.VMEM(normals.shape, F32),
             pltpu.SemaphoreType.DMA((4,)),
             pltpu.SemaphoreType.DMA((4,)),
+            pltpu.SemaphoreType.DMA((2,)),
         ],
         compiler_params=pltpu.CompilerParams(
             collective_id=0, has_side_effects=True, vmem_limit_bytes=VMEM_LIMIT
@@ -634,7 +649,7 @@
     return pl.pallas_call(
         sample_kernel,
         out_shape=shape(normals.shape, F32),
-        in_specs=[SMEM_SPEC] * 5 + [VMEM_SPEC] * 3,
+        in_specs=[SMEM_SPEC] * 4 + [VMEM_SPEC] * 2,
         out_specs=VMEM_SPEC,
         scratch_shapes=[
             pltpu.VMEM((2, K + 1, B, (K + 1) * B), F32),
@@ -669,7 +684,7 @@
             collective_id=1, has_side_effects=True, vmem_limit_bytes=VMEM_LIMIT
         ),
         name="sample",
-    )(key, rank_of_cell, out_key, my_slots, there, coords, near, draws)
+    )(key, rank_of_cell, out_key, there, near, draws)
 
 
 def solution(mesh):

time: 127 us -> 126 us (level)
  Pallas kernels: 123 us -> 121 us
    pallas_call x1, Pallas kernels: 97.9 us -> 96.5 us  [local(): pl.pallas_call(sample_kernel, out_shape=shape(normals.shape, F32), in_spe...]
    unnamed x10 -> x8, local copies, waits for them, and re-layouts: 3.49 us -> 2.79 us
where the time goes in v5:
time: 126 us; the launch traced here: 124 us
  Pallas kernels  121 us (96%)
  local copies, waits for them, and re-layouts  2.79 us (2%)
    pallas_call x1, Pallas kernels, local(): pl.pallas_call(sample_kernel, out_shape=shape(normals.shape, F32), in_spe...  96.5 us
    pallas_call x1, Pallas kernels, local(): pl.pallas_call(exchange_kernel, out_shape=(shape((2, 16, B), F32), shape(...  24.8 us
    unnamed x8, local copies, waits for them, and re-layouts  2.79 us

profile of v5, /device:TPU:1, one launch (start us, length us, event | category | flops | bytes accessed | tf_op | source)
XLA Modules:
  0.0 124.1 jit_solution(4874832118636701230)
XLA Ops:
  0.0 0.0 copy-start.2
  0.0 0.8 copy.5.neighbours_ref
  0.8 0.0 copy-done.2
  0.8 0.0 copy-start
  0.8 0.7 copy-done
  1.5 0.0 copy-start.1
  1.5 0.7 copy-done.1
  2.2 24.8 %exchange.1 = (f32[2,16,128]{2,1,0:T(8,128)S(1)}, s32[8,128]{1,0:T(8,128)S(1)}, f32[4,8,128]{2,1,0:T(8,128)S(1)}, s32[16]{0:T(128)S(1)}, s32[8]{0:T(128)S(1)}, /*index=5*/s32[8]{0:T(128)S(1)}) custom-call(s32[8]{0:T(128)S(1)} %copy-done.2, s32[8,4]{1,0:T(8,128)S(1)} %copy.5.neighbours_ref, f32[8,2,128]{2,1,0:T(2,128)S(1)} %copy-done.1, f32[4,1024]{1,0:T(4,128)S(1)} %copy-done), custom_call_target="tpu_custom_call" | custom-call | tf_op jit(solution)/shard_map/exchange/pallas_call | solution.py:616
  27.0 96.5 %sample.1 = f32[4,1024]{1,0:T(4,128)S(1)} custom-call(s32[8,128]{1,0:T(8,128)S(1)} %get-tuple-element.11.key_ref, s32[16]{0:T(128)S(1)} %get-tuple-element.12.rank_ref, s32[8]{0:T(128)S(1)} %get-tuple-element.13.out_key_ref, s32[8]{0:T(128)S(1)} %get-tuple-element.14.there_ref, f32[2,16,128]{2,1,0:T(8,128)S(1)} %get-tuple-element.15.near_ref, ...), custom_call_target="tpu_custom_call" | custom-call | tf_op jit(solution)/shard_map/sample/pallas_call | solution.py:649
  123.5 0.6 copy.7
Async XLA Ops:
  0.0 0.8 copy-start.2
  0.8 0.7 copy-start
  1.5 0.7 copy-start.1
